TPU v7x, 32 devices: a whole 2x2x4 slice. The times are simulated.
32 devices in a mesh: tm: 8 (over y, x, core), ops: 4 (over z).
Axes of the slice: x: 2, y: 2, z: 4, core: 2. Of those that a mesh axis runs over, the one named last changes fastest.
Arguments:
- node_blocks: bfloat16 [128, 384, 768], P(('tm', 'ops')), may hold values from -6 to 6
- first_pulls: int32 [32, 16], replicated, may hold values from 0 to 127, as said below
- first_left: int32 [32, 24], replicated, may hold values from 0 to 15
- first_right: int32 [32, 24], replicated, may hold values from 0 to 15
- first_live: int32 [32], replicated, may hold values from 1 to 24, as said below
- second_pulls: int32 [32, 16], replicated, may hold values from 0 to 767, as said below
- second_left: int32 [32, 16], replicated, may hold values from 0 to 15
- second_right: int32 [32, 16], replicated, may hold values from 0 to 15
- second_live: int32 [32], replicated, may hold values from 1 to 16, as said below
- diagram_ids: int32 [32, 16], replicated, may hold values from 0 to 31, as said below
- diagram_signs: int32 [32, 16], replicated, may hold values from -1 to 1, as said below
Outputs:
- diagrams: float32 [32, 384, 768], P(('tm', 'ops'))
Inputs may be any that keep to these rules, and one draw needn't show every extreme that they name: `first_pulls`: every node in row w belongs to a device with the same ops index as w. At most 2 entries of a row belong to any one device, and every row has a device with exactly 2. `first_live`: some worker has 24 pairs. `second_pulls`: each entry is an id h * 24 + p with p < first_live[h], where h is a device with the same tm index as w. At most 4 entries of a row belong to any one device h, and every row has a device with exactly 4. `second_live`: some worker has 16 pairs. `diagram_ids`: every diagram of row w is owned by a device with the same tm index as w. `diagram_signs`: each entry is +1 or -1.
All inputs are finite; a program needn't handle non-finite values.
Results may differ from a plain program's by a relative error of at most 0.004.
Values may be sent and summed in bfloat16 or wider, within the bound.
A program may use at most 128 MiB of HBM per device.

v0:
```python
import math

import jax
import jax.numpy as jnp
from jax import lax
from jax.sharding import PartitionSpec as P

DIAG_DEV = 1


def complex_product(first_block, second_block):
    rank_size = first_block.shape[0]
    second_real = second_block[:, :rank_size]
    second_imag = second_block[:, rank_size:]
    upper_half = jnp.concatenate([second_real, second_imag], axis=1)
    lower_half = jnp.concatenate([-second_imag, second_real], axis=1)
    stacked = jnp.concatenate([upper_half, lower_half], axis=0)
    return jnp.dot(first_block, stacked, preferred_element_type=jnp.float32)


def source_ranks(sources):
    length = sources.shape[-1]
    positions = jnp.arange(length)
    earlier = positions[:, None] > positions[None, :]
    same_source = sources[..., :, None] == sources[..., None, :]
    return jnp.sum(jnp.logical_and(same_source, earlier), axis=-1)


def pack_sends(blocks, sources, local_rows, own_index, slot_count):
    slot_ranks = source_ranks(sources)
    slot_ids = jnp.arange(slot_count)
    from_here = jnp.logical_and(
        (sources == own_index)[:, None, :], slot_ranks[:, None, :] == slot_ids[None, :, None]
    )
    chosen = jnp.sum(jnp.where(from_here, local_rows[:, None, :], 0), axis=-1).reshape(-1)
    filled = jnp.any(from_here, axis=-1).reshape(-1)
    picked = jnp.take(blocks, chosen, axis=0)
    return jnp.where(filled[:, None, None], picked, jnp.zeros_like(picked))


def unpack_received(received, own_sources, slot_count):
    positions = own_sources * slot_count + source_ranks(own_sources)
    return jnp.take(received, positions, axis=0)


def body(
    node_blocks,
    first_pulls,
    first_left,
    first_right,
    first_live,
    second_pulls,
    second_left,
    second_right,
    second_live,
    diagram_ids,
    diagram_signs,
):
    group_count = lax.axis_size("ops")
    time_index = lax.axis_index("tm")
    group_index = lax.axis_index("ops")
    worker = time_index * group_count + group_index
    held_nodes = node_blocks.shape[0]
    rank_size = node_blocks.shape[1]
    norm_factor = 1.0 / math.sqrt(2.0 * rank_size)
    first_cap = first_left.shape[1]
    first_reads = first_pulls.shape[1]
    second_reads = second_pulls.shape[1]
    block_shape = (rank_size, 2 * rank_size)
    own_pulls = first_pulls[worker]
    own_times = own_pulls // held_nodes // group_count
    column_pos = own_times * held_nodes + own_pulls % held_nodes
    empty_inputs = jnp.zeros((first_reads,) + block_shape, jnp.bfloat16)
    shard_rows = lax.all_gather(node_blocks, "tm", axis=0, tiled=True)
    piece_rows = shard_rows.shape[0]
    inside = jnp.logical_and(column_pos >= 0, column_pos < piece_rows)
    picked = jnp.take(shard_rows, jnp.clip(column_pos, 0, piece_rows - 1), axis=0)
    first_inputs = jnp.where(inside[:, None, None], picked, empty_inputs)
    own_left = first_left[worker]
    own_right = first_right[worker]

    def first_pair(pair_index, stored):
        product = complex_product(
            first_inputs[own_left[pair_index]], first_inputs[own_right[pair_index]]
        )
        return lax.dynamic_update_index_in_dim(
            stored, (product * norm_factor).astype(jnp.bfloat16), pair_index, 0
        )

    stored = lax.fori_loop(
        0, first_live[worker], first_pair, jnp.zeros((first_cap,) + block_shape, jnp.bfloat16)
    )
    second_slots = max(1, second_reads // group_count)
    row_workers = time_index * group_count + jnp.arange(group_count)
    row_pulls = jnp.take(second_pulls, row_workers, axis=0)
    row_groups = row_pulls // first_cap % group_count
    outgoing_products = pack_sends(
        stored, row_groups, row_pulls % first_cap, group_index, second_slots
    )
    arrived = lax.all_to_all(outgoing_products, "ops", split_axis=0, concat_axis=0, tiled=True)
    own_second = second_pulls[worker]
    second_inputs = unpack_received(arrived, own_second // first_cap % group_count, second_slots)
    pair_left = second_left[worker]
    pair_right = second_right[worker]
    targets = diagram_ids[worker] - time_index * group_count * DIAG_DEV
    weights = diagram_signs[worker].astype(jnp.float32) * norm_factor
    live_pairs = second_live[worker]

    def second_term(pair_index):
        product = complex_product(
            second_inputs[pair_left[pair_index]], second_inputs[pair_right[pair_index]]
        )
        return product * weights[pair_index]

    def second_pair(pair_index, partial_sum):
        return partial_sum.at[targets[pair_index]].add(second_term(pair_index))

    partial_sum = lax.fori_loop(
        0, live_pairs, second_pair, jnp.zeros((group_count * DIAG_DEV,) + block_shape, jnp.float32)
    )
    return lax.psum_scatter(partial_sum, "ops", scatter_dimension=0, tiled=True)


def solution(mesh):
    placed = (P(("tm", "ops"), None, None), P(), P(), P(), P(), P(), P(), P(), P(), P(), P())
    return jax.shard_map(
        body, mesh=mesh, in_specs=placed, out_specs=P(("tm", "ops"), None, None), check_vma=False
    )
```

profile of v0, /device:TPU:0, one launch (start us, length us, event | category | flops | bytes accessed | tf_op | source)
XLA Modules:
  0.0 838.3 jit_solution(7715150450191914720)
XLA Ops:
  13.8 96.9 %all-gather.2.cloned.1.call-done = bf16[32,384,768]{2,1,0:T(8,128)(2,1)} async-done(((bf16[4,384,768]{2,1,0:T(8,128)(2,1)}), bf16[32,384,768]{2,1,0:T(8,128)(2,1)}) %all-gather.2.cloned.1.call-update) | async-done | bytes 18874384 | tf_op jit(solution)/shard_map/all_gather | solution.py:74
  110.7 11.7 %gather_fusion.1 = bf16[16,384,768]{2,1,0:T(8,128)(2,1)} fusion(bf16[32,384,768]{2,1,0:T(8,128)(2,1)} %all-gather.2.cloned.1.call-done, s32[1024]{0:T(1024)S(1)} %pad_clamp_fusion.2), kind=kCustom, calls=%fused_computation.1 | custom fusion | bytes 18874432 | tf_op jit(solution)/shard_map/jit(_take)/gather | solution.py:77
  122.4 8.6 %select_select_fusion.1 = bf16[16,384,768]{2,1,0:T(8,128)(2,1)} fusion(bf16[16,384,768]{2,1,0:T(8,128)(2,1)} %gather_fusion.1, pred[16]{0:T(512)(128)(4,1)S(1)} %compare_and_fusion, pred[16]{0:T(512)(128)(4,1)S(1)} %get-tuple-element.129), kind=kLoop, calls=%fused_computation.36 | loop fusion | flops 9437184 | bytes 18874400 | tf_op jit(solution)/shard_map/jit(_where)/select_n | solution.py:78
  131.0 6.6 broadcast_in_dim.97
  137.5 85.6 %while.21 = (s32[]{:T(128)}, bf16[24,384,768]{2,1,0:T(8,128)(2,1)}, s32[]{:T(128)}, s32[24]{0:T(128)S(1)}, bf16[16,384,768]{2,1,0:T(8,128)(2,1)}, /*index=5*/s32...) while((s32[]{:T(128)}, bf16[24,384,768]{2,1,0:T(8,128)(2,1)}, s32[]{:T(128)}, s32[24]{0:T(128)S(1)}, ...), condition=%wide.region_5.6_spmd, body=%wide.region_4.5_spmd.sunk | while | flops 457261056 | bytes 4718831 | solution.py:90
  223.1 10.2 %gather_fusion.2 = bf16[16,384,768]{2,1,0:T(8,128)(2,1)} fusion(bf16[24,384,768]{2,1,0:T(8,128)(2,1)} %get-tuple-element.93, s32[1024]{0:T(1024)S(1)} %pad_clamp_fusion.1), kind=kCustom, calls=%fused_computation.2 | custom fusion | bytes 18874432 | tf_op jit(solution)/shard_map/jit(_take)/gather | solution.py:37
  233.4 8.3 select_select_fusion
  241.7 88.8 %all-to-all-start = ((bf16[16,384,768]{2,1,0:T(8,128)(2,1)}), bf16[16,384,768]{2,1,0:T(8,128)(2,1)}, u32[]{:S(2)}, u32[]{:S(2)}) async-start(bf16[16,384,768]{2,1,0:T(8,128)(2,1)} %select_select_fusion), calls=%async_computation | async-start | bytes 18874368 | tf_op jit(solution)/shard_map/all_to_all | solution.py:100
  331.9 158.2 %all-to-all-done = bf16[16,384,768]{2,1,0:T(8,128)(2,1)} async-done(((bf16[16,384,768]{2,1,0:T(8,128)(2,1)}), bf16[16,384,768]{2,1,0:T(8,128)(2,1)}, u32[]{:S(2)}, u32[]{:S(2)}) %all-to-all-start) | async-done | bytes 9437216 | tf_op jit(solution)/shard_map/all_to_all | solution.py:100
  490.1 9.0 %gather_fusion.3 = bf16[16,384,768]{2,1,0:T(8,128)(2,1)} fusion(bf16[16,384,768]{2,1,0:T(8,128)(2,1)} %all-to-all-done, s32[1024]{0:T(1024)S(1)} %pad_clamp_fusion), kind=kCustom, calls=%fused_computation.3 | custom fusion | bytes 18874432 | tf_op jit(solution)/shard_map/jit(_take)/gather | solution.py:43
  499.1 8.3 broadcast_select_fusion
  509.9 180.7 %while.22 = (s32[]{:T(128)}, f32[4,384,768]{2,1,0:T(8,128)}, s32[]{:T(128)}, s32[16]{0:T(128)S(1)}, s32[16]{0:T(128)S(1)}, /*index=5*/bf16[16,384,768]{2,1,0:T(8...) while((s32[]{:T(128)}, f32[4,384,768]{2,1,0:T(8,128)}, ...), condition=%wide.region_8.9_spmd, body=%wide.region_6.8_spmd.sunk | while | flops 457556000 | bytes 6489946 | solution.py:118
  520.5 4.4 fusion.55
  535.6 4.4 fusion.55
  550.6 4.4 fusion.55
  565.6 4.4 fusion.55
  595.6 4.4 fusion.55
  610.6 4.4 fusion.55
  625.7 4.4 fusion.55
  640.7 4.4 fusion.55
  655.7 4.4 fusion.55
  670.7 4.4 fusion.55
  685.7 4.4 fusion.55
  690.7 140.8 %reduce-scatter.2.cloned.1.call-done = f32[1,384,768]{2,1,0:T(8,128)} async-done(((f32[4,384,768]{2,1,0:T(8,128)}), f32[1,384,768]{2,1,0:T(8,128)}) %reduce-scatter.2.cloned.1.call-update) | async-done | bytes 1179664 | tf_op jit(solution)/shard_map/reduce_scatter | solution.py:121
  (181 shorter events, 113.1 us)
Async XLA Ops:
  6.5 104.2 %all-gather.2.cloned.1.call-start = ((), (), s32[]{:S(2)}) async-start(), calls=%async_computation.2 | async-start | bytes 21233664 | tf_op jit(solution)/shard_map/all_gather | solution.py:74
  241.7 88.8 %copy-start.5 = (s32[32]{0:T(128)S(1)}, s32[32]{0:T(128)}, u32[]{:S(2)}) copy-start(s32[32]{0:T(128)} %param.25) | copy-start | bytes 388
  241.7 89.4 %copy-start.1 = (s32[32,16]{0,1:T(8,128)S(1)}, s32[32,16]{0,1:T(8,128)}, u32[]{:S(2)}) copy-start(s32[32,16]{0,1:T(8,128)} %param.26) | copy-start | bytes 6148
  241.7 89.6 %copy-start.2 = (s32[32,16]{0,1:T(8,128)S(1)}, s32[32,16]{0,1:T(8,128)}, u32[]{:S(2)}) copy-start(s32[32,16]{0,1:T(8,128)} %param.27) | copy-start | bytes 6148
  241.7 89.8 %copy-start.3 = (s32[32,16]{0,1:T(8,128)S(1)}, s32[32,16]{0,1:T(8,128)}, u32[]{:S(2)}) copy-start(s32[32,16]{0,1:T(8,128)} %param.24) | copy-start | bytes 6148
  241.7 89.8 %copy-start.4 = (s32[32,16]{0,1:T(8,128)S(1)}, s32[32,16]{0,1:T(8,128)}, u32[]{:S(2)}) copy-start(s32[32,16]{0,1:T(8,128)} %param.23) | copy-start | bytes 6148
  241.7 248.4 %all-to-all-start = ((bf16[16,384,768]{2,1,0:T(8,128)(2,1)}), bf16[16,384,768]{2,1,0:T(8,128)(2,1)}, u32[]{:S(2)}, u32[]{:S(2)}) async-start(bf16[16,384,768]{2,1,0:T(8,128)(2,1)} %select_select_fusion), calls=%async_computation | async-start | bytes 18874368 | tf_op jit(solution)/shard_map/all_to_all | solution.py:100
  330.5 501.0 %reduce-scatter.2.cloned.1.call-start = ((), (), s32[]{:S(2)}) async-start(), calls=%async_computation.3 | async-start | bytes 5898240 | tf_op jit(solution)/shard_map/reduce_scatter | solution.py:121
  499.1 10.8 %copy-start = (s32[3]{0:T(128)S(1)}, s32[3]{0:T(128)}, u32[]{:S(2)}) copy-start(s32[3]{0:T(128)} %constant.176.clone.1) | copy-start | bytes 40
Sparse Core Ops, SparseCore 0:
  9.2 101.4 all-gather.1
  690.8 140.5 reduce-scatter.1
where the time goes:
time: 848 us; the launch traced here: 838 us
  waiting for transfers between devices  397 us (47%)
  loops' own time  116 us (14%)
  local copies, waits for them, and re-layouts  109 us (13%)
  starting transfers between devices  88.8 us (10%)
  matrix products  75.6 us (9%)
  other arithmetic  38.9 us (5%)
  between operations  13.5 us (2%)
    all_to_all x1, waiting for transfers between devices, body(): lax.all_to_all(outgoing_products, 'ops', split_axis=0, concat_axis=0, til...  158 us
    reduce_scatter x1, waiting for transfers between devices, body(): return lax.psum_scatter(partial_sum, 'ops', scatter_dimension=0, tiled=True)  141 us
    all_gather x1, waiting for transfers between devices, body(): shard_rows = lax.all_gather(node_blocks, 'tm', axis=0, tiled=True)  96.9 us
    all_to_all x1, starting transfers between devices, body(): lax.all_to_all(outgoing_products, 'ops', split_axis=0, concat_axis=0, til...  88.8 us
    dot_general x21, matrix products, complex_product(): return jnp.dot(first_block, stacked, preferred_element_type=jnp.float32)  75.6 us
    another operation x1, loops' own time, body(): lax.fori_loop(0, live_pairs, second_pair, jnp.zeros((group_count * DIAG_D...  74.5 us
    another operation x1, loops' own time, body(): lax.fori_loop(0, first_live[worker], first_pair, jnp.zeros((first_cap,) +...  41.3 us
  transfers between devices with their start and end apart: 3, of which 3 were waited for; matrix products, arithmetic and copies ran while one was open for 1% of the time, Pallas kernels for 0%

commit v1 on v0

v1 whole, which is shorter than its diff:
```python
import math

import jax
import jax.numpy as jnp
from jax import lax
from jax.experimental import pallas as pl
from jax.experimental.pallas import tpu as pltpu
from jax.sharding import PartitionSpec as P

DIAG_DEV = 1
VMEM_BYTES = 48 * 1024 * 1024


def complex_product(first_block, second_block, stacked):
    rank_size = first_block.shape[0]
    stacked[:rank_size, :] = second_block
    stacked[rank_size:, :rank_size] = -second_block[:, rank_size:]
    stacked[rank_size:, rank_size:] = second_block[:, :rank_size]
    return jnp.dot(first_block, stacked[...], preferred_element_type=jnp.float32)


def first_kernel(norm_factor, left, right, used, a_ref, b_ref, out_ref, stacked):
    @pl.when(used[pl.program_id(0)] > 0)
    def _():
        product = complex_product(a_ref[0], b_ref[0], stacked)
        out_ref[0] = (product * norm_factor).astype(out_ref.dtype)


def second_kernel(left, right, target, sign, live, norm, a_ref, b_ref, out_ref, total, stacked):
    step = pl.program_id(0)

    @pl.when(step == 0)
    def _():
        total[...] = jnp.zeros_like(total)

    @pl.when(step < live[0])
    def _():
        weight = sign[step].astype(jnp.float32) * norm
        total[target[step]] += complex_product(a_ref[0], b_ref[0], stacked) * weight

    @pl.when(step == pl.num_programs(0) - 1)
    def _():
        out_ref[...] = total[...].astype(out_ref.dtype)


def pair_specs(rank_size):
    block = (1, rank_size, 2 * rank_size)
    return [
        pl.BlockSpec(block, lambda s, left, right, *_: (left[s], 0, 0)),
        pl.BlockSpec(block, lambda s, left, right, *_: (right[s], 0, 0)),
    ]


def first_products(blocks, left, right, used, norm_factor):
    steps = left.shape[0]
    rank_size = blocks.shape[1]
    block = (1, rank_size, 2 * rank_size)
    return pl.pallas_call(
        lambda *refs: first_kernel(norm_factor, *refs),
        grid_spec=pltpu.PrefetchScalarGridSpec(
            num_scalar_prefetch=3,
            grid=(steps,),
            in_specs=pair_specs(rank_size),
            out_specs=pl.BlockSpec(block, lambda s, *_: (s, 0, 0)),
            scratch_shapes=[pltpu.VMEM((2 * rank_size, 2 * rank_size), jnp.bfloat16)],
        ),
        out_shape=jax.ShapeDtypeStruct((steps,) + block[1:], jnp.bfloat16),
        compiler_params=pltpu.CompilerParams(vmem_limit_bytes=VMEM_BYTES),
        name="first_section",
    )(left, right, used, blocks, blocks)


def second_sums(blocks, left, right, target, sign, live, norm_factor, diagram_count):
    steps = left.shape[0]
    rank_size = blocks.shape[1]
    shape = (diagram_count, rank_size, 2 * rank_size)
    return pl.pallas_call(
        lambda left, right, target, sign, live, *refs: second_kernel(
            left, right, target, sign, live, norm_factor, *refs
        ),
        grid_spec=pltpu.PrefetchScalarGridSpec(
            num_scalar_prefetch=5,
            grid=(steps,),
            in_specs=pair_specs(rank_size),
            out_specs=pl.BlockSpec(shape, lambda s, *_: (0, 0, 0)),
            scratch_shapes=[
                pltpu.VMEM(shape, jnp.float32),
                pltpu.VMEM((2 * rank_size, 2 * rank_size), jnp.bfloat16),
            ],
        ),
        out_shape=jax.ShapeDtypeStruct(shape, jnp.bfloat16),
        compiler_params=pltpu.CompilerParams(vmem_limit_bytes=VMEM_BYTES),
        name="second_section",
    )(left, right, target, sign, live, blocks, blocks)


def source_ranks(sources):
    length = sources.shape[-1]
    positions = jnp.arange(length)
    earlier = positions[:, None] > positions[None, :]
    same_source = sources[..., :, None] == sources[..., None, :]
    return jnp.sum(jnp.logical_and(same_source, earlier), axis=-1)


def pick(table, index):
    match = index[..., None] == jnp.arange(table.shape[0])
    return jnp.sum(jnp.where(match, table, 0), axis=-1)


def body(
    node_blocks,
    first_pulls,
    first_left,
    first_right,
    first_live,
    second_pulls,
    second_left,
    second_right,
    second_live,
    diagram_ids,
    diagram_signs,
):
    group_count = lax.axis_size("ops")
    time_index = lax.axis_index("tm")
    group_index = lax.axis_index("ops")
    worker = time_index * group_count + group_index
    held_nodes = node_blocks.shape[0]
    rank_size = node_blocks.shape[1]
    norm_factor = 1.0 / math.sqrt(2.0 * rank_size)
    first_cap = first_left.shape[1]
    second_reads = second_pulls.shape[1]
    second_cap = second_left.shape[1]
    second_slots = max(1, second_reads // group_count)

    shard_rows = lax.all_gather(node_blocks, "tm", axis=0, tiled=True)

    def own_rows(table):
        return lax.dynamic_slice_in_dim(table, time_index * group_count, group_count, 0)

    own_pulls = first_pulls[worker]
    column_pos = own_pulls // held_nodes // group_count * held_nodes + own_pulls % held_nodes
    row_pulls = own_rows(second_pulls)
    row_sources = row_pulls // first_cap % group_count
    ranks = source_ranks(row_sources)
    from_here = jnp.logical_and(
        (row_sources == group_index)[:, None, :],
        ranks[:, None, :] == jnp.arange(second_slots)[None, :, None],
    )
    pair_ids = jnp.sum(jnp.where(from_here, (row_pulls % first_cap)[:, None, :], 0), axis=-1)
    live = jnp.arange(second_cap)[None, :] < own_rows(second_live)[:, None]
    spots = jnp.arange(second_reads)[None, None, :]
    read = jnp.logical_or(
        own_rows(second_left)[:, :, None] == spots, own_rows(second_right)[:, :, None] == spots
    )
    read = jnp.any(jnp.logical_and(read, live[:, :, None]), axis=1)
    used = jnp.any(jnp.logical_and(from_here, read[:, None, :]), axis=-1)
    pair_ids = pair_ids.reshape(-1)
    left_nodes = pick(column_pos, pick(first_left[worker], pair_ids))
    right_nodes = pick(column_pos, pick(first_right[worker], pair_ids))
    own_sources = lax.dynamic_index_in_dim(row_sources, group_index, 0, keepdims=False)
    own_ranks = lax.dynamic_index_in_dim(ranks, group_index, 0, keepdims=False)
    places = own_sources * second_slots + own_ranks
    second_left_at = pick(places, second_left[worker])
    second_right_at = pick(places, second_right[worker])
    targets = diagram_ids[worker] - time_index * group_count * DIAG_DEV

    outgoing = first_products(
        shard_rows, left_nodes, right_nodes, used.reshape(-1).astype(jnp.int32), norm_factor
    )
    arrived = lax.all_to_all(outgoing, "ops", split_axis=0, concat_axis=0, tiled=True)
    partial_sum = second_sums(
        arrived,
        second_left_at,
        second_right_at,
        targets,
        diagram_signs[worker],
        second_live[worker][None],
        norm_factor,
        group_count * DIAG_DEV,
    )
    terms = lax.all_to_all(partial_sum, "ops", split_axis=0, concat_axis=0, tiled=True)
    terms = terms.reshape((group_count, DIAG_DEV) + terms.shape[1:])
    return jnp.sum(terms.astype(jnp.float32), axis=0)


def solution(mesh):
    placed = (P(("tm", "ops"), None, None), P(), P(), P(), P(), P(), P(), P(), P(), P(), P())
    return jax.shard_map(
        body, mesh=mesh, in_specs=placed, out_specs=P(("tm", "ops"), None, None), check_vma=False
    )
```

time: 848 us -> 421 us (0.50); the launches traced: 838 us -> 421 us
  loops' own time: 116 us -> 0 us
  local copies, waits for them, and re-layouts: 109 us -> 1.81 us
  waiting for transfers between devices: 397 us -> 307 us
  starting transfers between devices: 88.8 us -> 5.98 us
  matrix products: 75.6 us -> 0 us
  blocking collectives: 0 us -> 56.4 us
  other arithmetic: 38.9 us -> 2.86 us
  Pallas kernels: 0 us -> 33.4 us
    reduce_scatter x1 -> x0, waiting for transfers between devices: 141 us -> none  [body(): return lax.psum_scatter(partial_sum, 'ops', scatter_dimension=0, tiled=True)]
    another operation x2 -> x0, loops' own time: 116 us -> none  [the longest x1 74.5 us: body(): lax.fori_loop(0, live_pairs, second_pair, jnp.zeros((group_count * DIAG_D...]
    all_to_all x1, starting transfers between devices: 88.8 us -> 5.94 us  [body(): lax.all_to_all(outgoing, 'ops', split_axis=0, concat_axis=0, tiled=True)]
    dot_general x21 -> x0, matrix products: 75.6 us -> none  [complex_product(): return jnp.dot(first_block, stacked, preferred_element_type=jnp.float32)]
    all_to_all x0 -> x1, blocking collectives: none -> 56.4 us  [body(): lax.all_to_all(partial_sum, 'ops', split_axis=0, concat_axis=0, tiled=True)]
    all_to_all x1, waiting for transfers between devices: 158 us -> 205 us  [body(): lax.all_to_all(outgoing, 'ops', split_axis=0, concat_axis=0, tiled=True)]
    dynamic_slice x70 -> x9, local copies, waits for them, and re-layouts: 44.1 us -> 1.53 us  [the longest x1 0.59 us: body(): second_live[worker][None]]
    pallas_call x0 -> x2, Pallas kernels: none -> 33.4 us  [the longest x1 18.1 us: first_products(): pl.pallas_call(lambda *refs: first_kernel(norm_factor, *refs), grid_spec=...]
  transfers between devices with their start and end apart: 3 -> 2, of which waited for: 3 -> 2; matrix products, arithmetic and copies ran while one was open for 1% -> 1% of each run, Pallas kernels for 0% -> 0%
where the time goes in v1:
time: 421 us
  waiting for transfers between devices  307 us (73%)
  blocking collectives  56.4 us (13%)
  Pallas kernels  33.4 us (8%)
  between operations  13.5 us (3%)
  starting transfers between devices  5.98 us (1%)
    all_to_all x1, waiting for transfers between devices, body(): lax.all_to_all(outgoing, 'ops', split_axis=0, concat_axis=0, tiled=True)  205 us
    all_gather x1, waiting for transfers between devices, body(): shard_rows = lax.all_gather(node_blocks, 'tm', axis=0, tiled=True)  101 us
    all_to_all x1, blocking collectives, body(): lax.all_to_all(partial_sum, 'ops', split_axis=0, concat_axis=0, tiled=True)  56.4 us
    pallas_call x1, Pallas kernels, first_products(): pl.pallas_call(lambda *refs: first_kernel(norm_factor, *refs), grid_spec=...  18.1 us
    pallas_call x1, Pallas kernels, second_sums(): pl.pallas_call(lambda left, right, target, sign, live, *refs: second_kern...  15.3 us
  transfers between devices with their start and end apart: 2, of which 2 were waited for; matrix products, arithmetic and copies ran while one was open for 1% of the time, Pallas kernels for 0%

profile of v1, /device:TPU:0, one launch (start us, length us, event | category | flops | bytes accessed | tf_op | source)
XLA Modules:
  0.0 420.6 jit_solution(11671942558698527900)
XLA Ops:
  6.6 0.7 all-gather.2.cloned.1.call-update
  7.5 0.1 copy.35
  7.6 0.2 convert_reduce_fusion.1
  7.8 0.2 select_reduce_fusion.4
  8.0 0.1 eq.160
  8.1 0.1 copy.34
  8.4 0.1 fusion.2
  8.5 0.2 and_reduce_fusion
  8.7 0.1 reshape.57.refs_2_
  8.7 0.2 dynamic-slice_reduce_fusion.2
  9.0 0.2 dynamic-slice_reduce_fusion
  9.1 0.2 select_reduce_fusion.1
  9.4 0.2 select_reduce_fusion
  9.5 101.2 %all-gather.2.cloned.1.call-done.refs_3_.refs_4_ = bf16[32,384,768]{2,1,0:T(8,128)(2,1)} async-done(((bf16[4,384,768]{2,1,0:T(8,128)(2,1)}), bf16[32,384,768]{2,1,0:T(8,128)(2,1)}) %all-gather.2.cloned.1.call-update) | async-done | bytes 18874384 | tf_op jit(solution)/shard_map/all_gather | solution.py:135
  110.7 18.1 %first_section.1 = bf16[16,384,768]{2,1,0:T(8,128)(2,1)} custom-call(s32[16]{0:T(128)S(1)} %get-tuple-element.6.refs_0_, s32[16]{0:T(128)S(1)} %get-tuple-element.5.refs_1_, s32[16]{0:T(128)S(1)} %reshape.57.refs_2_, bf16[32,384,768]{2,1,0:T(8,128)(2,1)} %all-gather.2.cloned.1.call-done.refs_3_.refs_4_, ...), custom_call_target="tpu_custom_call" | custom-call | tf_op jit(solution)/shard_map/first_section/pallas_call | solution.py:58
  128.9 5.9 %all-to-all-start = ((bf16[16,384,768]{2,1,0:T(8,128)(2,1)}), bf16[16,384,768]{2,1,0:T(8,128)(2,1)}, u32[]{:S(2)}, u32[]{:S(2)}) async-start(bf16[16,384,768]{2,1,0:T(8,128)(2,1)} %first_section.1), calls=%async_computation | async-start | bytes 18874368 | tf_op jit(solution)/shard_map/all_to_all | solution.py:170
  134.8 0.6 dynamic_slice.50.live
  135.4 0.2 dynamic-slice_reduce_fusion.5
  135.6 0.2 dynamic-slice_reduce_fusion.3
  135.8 0.2 select_reduce_fusion.5
  136.0 204.8 %all-to-all-done.refs_0_.refs_1_ = bf16[16,384,768]{2,1,0:T(8,128)(2,1)} async-done(((bf16[16,384,768]{2,1,0:T(8,128)(2,1)}), bf16[16,384,768]{2,1,0:T(8,128)(2,1)}, u32[]{:S(2)}, u32[]{:S(2)}) %all-to-all-start) | async-done | bytes 9437216 | tf_op jit(solution)/shard_map/all_to_all | solution.py:170
  340.8 15.3 %second_section.1 = bf16[4,384,768]{2,1,0:T(8,128)(2,1)S(1)} custom-call(s32[16]{0:T(128)S(1)} %get-tuple-element.10.left, s32[16]{0:T(128)S(1)} %get-tuple-element.9.right, s32[16]{0:T(128)S(1)} %get-tuple-element.18.target, s32[16]{0:T(128)S(1)} %get-tuple-element.17.sign, s32[1]{0:T(128)} %dynamic_slice.50.live, ...), custom_call_target="tpu_custom_call" | custom-call | tf_op jit(solution)/shard_map/second_section/pallas_call | solution.py:77
  356.1 56.4 %all_to_all.10 = bf16[4,384,768]{2,1,0:T(8,128)(2,1)S(1)} all-to-all(bf16[4,384,768]{2,1,0:T(8,128)(2,1)S(1)} %second_section.1), channel_id=1, replica_groups=mesh['tm'=8,'ops'=4] {'ops'}, dimensions={0} | all-to-all | bytes 4718592 | tf_op jit(solution)/shard_map/all_to_all | solution.py:181
  412.5 1.3 convert_reduce_fusion
  (30 shorter events, 0.5 us)
Async XLA Ops:
  6.5 0.9 copy-start
  6.5 0.8 copy-start.8
  6.5 1.5 copy-start.1
  6.5 1.5 copy-start.2
  6.5 2.2 copy-start.5
  6.5 2.4 copy-start.3
  6.6 2.4 copy-start.4
  6.6 104.2 %all-gather.2.cloned.1.call-start = ((), (), s32[]{:S(2)}) async-start(), calls=%async_computation.2 | async-start | bytes 21233664 | tf_op jit(solution)/shard_map/all_gather | solution.py:135
  128.9 6.7 %copy-start.6 = (s32[32,16]{0,1:T(8,128)S(1)}, s32[32,16]{0,1:T(8,128)}, u32[]{:S(2)}) copy-start(s32[32,16]{0,1:T(8,128)} %param.20) | copy-start | bytes 6148
  128.9 6.7 %copy-start.7 = (s32[32,16]{0,1:T(8,128)S(1)}, s32[32,16]{0,1:T(8,128)}, u32[]{:S(2)}) copy-start(s32[32,16]{0,1:T(8,128)} %param.19) | copy-start | bytes 6148
  128.9 211.9 %all-to-all-start = ((bf16[16,384,768]{2,1,0:T(8,128)(2,1)}), bf16[16,384,768]{2,1,0:T(8,128)(2,1)}, u32[]{:S(2)}, u32[]{:S(2)}) async-start(bf16[16,384,768]{2,1,0:T(8,128)(2,1)} %first_section.1), calls=%async_computation | async-start | bytes 18874368 | tf_op jit(solution)/shard_map/all_to_all | solution.py:170
Sparse Core Ops, SparseCore 0:
  9.3 101.4 all-gather.1

commit v2 on v1

v2 whole, which is shorter than its diff:
```python
import math

import jax
import jax.numpy as jnp
from jax import lax
from jax.experimental import pallas as pl
from jax.experimental.pallas import tpu as pltpu
from jax.sharding import PartitionSpec as P

DIAG_DEV = 1
VMEM_BYTES = 48 * 1024 * 1024


def complex_product(first_block, second_block, stacked):
    rank_size = first_block.shape[0]
    stacked[:rank_size, :] = second_block
    stacked[rank_size:, :rank_size] = -second_block[:, rank_size:]
    stacked[rank_size:, rank_size:] = second_block[:, :rank_size]
    return jnp.dot(first_block, stacked[...], preferred_element_type=jnp.float32)


def first_kernel(norm_factor, left, right, used, a_ref, b_ref, out_ref, stacked):
    @pl.when(used[pl.program_id(0)] > 0)
    def _():
        product = complex_product(a_ref[0], b_ref[0], stacked)
        out_ref[0] = (product * norm_factor).astype(out_ref.dtype)


def second_kernel(region_count, norm, left, right, target, sign, live, *refs):
    regions = refs[:region_count]
    out_ref, held, total, stacked, arrivals = refs[region_count:]
    slots = regions[0].shape[0]
    copies = [
        pltpu.make_async_copy(regions[k], held.at[pl.ds(k * slots, slots)], arrivals.at[k])
        for k in range(region_count)
    ]
    for copy in copies:
        copy.start()
    total[...] = jnp.zeros_like(total)
    for copy in copies:
        copy.wait()

    @pl.loop(0, live[0])
    def _(step):
        weight = sign[step].astype(jnp.float32) * norm
        product = complex_product(held[left[step]], held[right[step]], stacked)
        total[target[step]] += product * weight

    out_ref[...] = total[...].astype(out_ref.dtype)


def product_cost(count, rank_size):
    return pl.CostEstimate(
        flops=16 * count * rank_size**3 // 2,
        bytes_accessed=12 * count * rank_size**2,
        transcendentals=0,
    )


def first_products(blocks, left, right, used, norm_factor):
    steps = left.shape[0]
    rank_size = blocks.shape[1]
    block = (1, rank_size, 2 * rank_size)
    return pl.pallas_call(
        lambda *refs: first_kernel(norm_factor, *refs),
        grid_spec=pltpu.PrefetchScalarGridSpec(
            num_scalar_prefetch=3,
            grid=(steps,),
            in_specs=[
                pl.BlockSpec(block, lambda s, left, right, used: (left[s], 0, 0)),
                pl.BlockSpec(block, lambda s, left, right, used: (right[s], 0, 0)),
            ],
            out_specs=pl.BlockSpec(block, lambda s, *_: (s, 0, 0)),
            scratch_shapes=[pltpu.VMEM((2 * rank_size, 2 * rank_size), jnp.bfloat16)],
        ),
        out_shape=jax.ShapeDtypeStruct((steps,) + block[1:], jnp.bfloat16),
        compiler_params=pltpu.CompilerParams(vmem_limit_bytes=VMEM_BYTES),
        cost_estimate=product_cost(steps, rank_size),
        name="first_section",
    )(left, right, used, blocks, blocks)


def second_sums(regions, left, right, target, sign, live, norm_factor, diagram_count):
    steps = left.shape[0]
    slots, rank_size, width = regions[0].shape
    shape = (diagram_count, rank_size, width)
    return pl.pallas_call(
        lambda *refs: second_kernel(len(regions), norm_factor, *refs),
        in_specs=[pl.BlockSpec(memory_space=pltpu.SMEM)] * 5
        + [pl.BlockSpec(memory_space=pl.ANY)] * len(regions),
        out_specs=pl.BlockSpec(memory_space=pltpu.VMEM),
        scratch_shapes=[
            pltpu.VMEM((len(regions) * slots, rank_size, width), jnp.bfloat16),
            pltpu.VMEM(shape, jnp.float32),
            pltpu.VMEM((2 * rank_size, width), jnp.bfloat16),
            pltpu.SemaphoreType.DMA((len(regions),)),
        ],
        out_shape=jax.ShapeDtypeStruct(shape, jnp.bfloat16),
        compiler_params=pltpu.CompilerParams(vmem_limit_bytes=VMEM_BYTES),
        cost_estimate=product_cost(steps, rank_size),
        name="second_section",
    )(left, right, target, sign, live, *regions)


def source_ranks(sources):
    length = sources.shape[-1]
    positions = jnp.arange(length)
    earlier = positions[:, None] > positions[None, :]
    same_source = sources[..., :, None] == sources[..., None, :]
    return jnp.sum(jnp.logical_and(same_source, earlier), axis=-1)


def pick(table, index):
    match = index[..., None] == jnp.arange(table.shape[0])
    return jnp.sum(jnp.where(match, table, 0), axis=-1)


def body(
    node_blocks,
    first_pulls,
    first_left,
    first_right,
    first_live,
    second_pulls,
    second_left,
    second_right,
    second_live,
    diagram_ids,
    diagram_signs,
):
    group_count = lax.axis_size("ops")
    time_index = lax.axis_index("tm")
    group_index = lax.axis_index("ops")
    worker = time_index * group_count + group_index
    held_nodes = node_blocks.shape[0]
    rank_size = node_blocks.shape[1]
    norm_factor = 1.0 / math.sqrt(2.0 * rank_size)
    first_cap = first_left.shape[1]
    second_reads = second_pulls.shape[1]
    second_cap = second_left.shape[1]
    second_slots = max(1, second_reads // group_count)
    half = group_count // 2

    def far_of(group):
        return 0 if group >= half else group_count - 1

    far_index = jnp.where(group_index >= half, 0, group_count - 1)
    near_rows = lax.all_gather(node_blocks, "tm", axis=0, tiled=True)
    far_nodes = None
    for step in range(half):
        crossing = [(0, half + step), (group_count - 1, half - 1 - step)]
        came = lax.ppermute(node_blocks, "ops", crossing)
        takes = jnp.logical_or(group_index == half + step, group_index == half - 1 - step)
        far_nodes = came if far_nodes is None else jnp.where(takes, came, far_nodes)
    far_rows = lax.all_gather(far_nodes, "tm", axis=0, tiled=True)

    def own_rows(table):
        return lax.dynamic_slice_in_dim(table, time_index * group_count, group_count, 0)

    def turned(rows):
        return lax.dynamic_slice_in_dim(
            jnp.concatenate([rows, rows], axis=0), group_index, group_count, 0
        )

    row_start = time_index * group_count
    row_pulls = own_rows(second_pulls)
    row_sources = row_pulls // first_cap % group_count
    row_pairs = row_pulls % first_cap
    ranks = source_ranks(row_sources)
    live = jnp.arange(second_cap)[None, :] < own_rows(second_live)[:, None]
    spots = jnp.arange(second_reads)[None, None, :]
    read = jnp.logical_or(
        own_rows(second_left)[:, :, None] == spots, own_rows(second_right)[:, :, None] == spots
    )
    read = jnp.any(jnp.logical_and(read, live[:, :, None]), axis=1)
    slot_ids = jnp.arange(second_slots)[None, :, None]

    def slots_of(sources, source, pairs, slot_ranks, reads):
        chosen = jnp.logical_and((sources == source)[:, None, :], slot_ranks[:, None, :] == slot_ids)
        pair_ids = jnp.sum(jnp.where(chosen, pairs[:, None, :], 0), axis=-1)
        used = jnp.any(jnp.logical_and(chosen, reads[:, None, :]), axis=-1)
        return pair_ids, used.astype(jnp.int32)

    def factors(holder, pair_ids):
        pulls = first_pulls[holder]
        column_pos = pulls // held_nodes // group_count * held_nodes + pulls % held_nodes
        return (
            pick(column_pos, pick(first_left[holder], pair_ids)),
            pick(column_pos, pick(first_right[holder], pair_ids)),
        )

    pair_ids, used = slots_of(
        turned(row_sources), group_index, turned(row_pairs), turned(ranks), turned(read)
    )
    readers = (group_index + jnp.arange(group_count)) % group_count
    apart = jnp.where(readers >= half, 0, group_count - 1) == group_index
    used = jnp.where(apart[:, None], 0, used)
    left_nodes, right_nodes = factors(worker, pair_ids)

    def own_row(rows):
        return lax.dynamic_slice_in_dim(rows, group_index, 1, 0)

    own_sources = own_row(row_sources)
    far_ids, far_used = slots_of(
        own_sources, far_index, own_row(row_pairs), own_row(ranks), own_row(read)
    )
    far_left, far_right = factors(row_start + far_index, far_ids)
    region = jnp.where(
        own_sources == far_index,
        group_count,
        (group_index - own_sources + group_count) % group_count,
    )
    places = (region * second_slots + own_row(ranks))[0]
    second_left_at = pick(places, second_left[worker])
    second_right_at = pick(places, second_right[worker])
    targets = diagram_ids[worker] - row_start * DIAG_DEV

    def near_products(turn):
        return first_products(
            near_rows, left_nodes[turn], right_nodes[turn], used[turn], norm_factor
        )

    regions = [None] * (group_count + 1)
    for turn in sorted(range(1, group_count), key=lambda j: -min(j, group_count - j)):
        pairs = [
            (source, (source + turn) % group_count)
            for source in range(group_count)
            if far_of((source + turn) % group_count) != source
        ]
        if pairs:
            regions[turn] = lax.ppermute(near_products(turn), "ops", pairs)
    regions[0] = near_products(0)
    regions[group_count] = first_products(
        far_rows, far_left[0], far_right[0], far_used[0], norm_factor
    )
    regions = [regions[0] if block is None else block for block in regions]
    partial_sum = second_sums(
        regions,
        second_left_at,
        second_right_at,
        targets,
        diagram_signs[worker],
        second_live[worker][None],
        norm_factor,
        group_count * DIAG_DEV,
    )
    terms = lax.all_to_all(partial_sum, "ops", split_axis=0, concat_axis=0, tiled=True)
    terms = terms.reshape((group_count, DIAG_DEV) + terms.shape[1:])
    return jnp.sum(terms.astype(jnp.float32), axis=0)


def solution(mesh):
    placed = (P(("tm", "ops"), None, None), P(), P(), P(), P(), P(), P(), P(), P(), P(), P())
    return jax.shard_map(
        body, mesh=mesh, in_specs=placed, out_specs=P(("tm", "ops"), None, None), check_vma=False
    )
```

time: 421 us -> 317 us (0.75)
  waiting for transfers between devices: 307 us -> 186 us
  starting transfers between devices: 5.98 us -> 14.6 us
  blocking collectives: 56.4 us -> 49.4 us
  Pallas kernels: 33.4 us -> 38.2 us
  other arithmetic: 2.86 us -> 7.39 us
    all_to_all x1 -> x0, waiting for transfers between devices: 205 us -> none  [body(): lax.all_to_all(outgoing, 'ops', split_axis=0, concat_axis=0, tiled=True)]
    ppermute x0 -> x5, waiting for transfers between devices: none -> 115 us  [the longest x2 99.7 us: body(): came = lax.ppermute(node_blocks, 'ops', crossing)]
    all_gather x1 -> x2, waiting for transfers between devices: 101 us -> 70 us  [the longest x1 69.9 us: body(): far_rows = lax.all_gather(far_nodes, 'tm', axis=0, tiled=True)]
    ppermute x0 -> x5, starting transfers between devices: none -> 14.6 us  [the longest x2 9.35 us: body(): came = lax.ppermute(node_blocks, 'ops', crossing)]
    all_to_all x1, blocking collectives: 56.4 us -> 49.4 us  [body(): lax.all_to_all(partial_sum, 'ops', split_axis=0, concat_axis=0, tiled=True)]
    all_to_all x1 -> x0, starting transfers between devices: 5.94 us -> none  [body(): lax.all_to_all(outgoing, 'ops', split_axis=0, concat_axis=0, tiled=True)]
    pallas_call x1 -> x5, Pallas kernels: 18.1 us -> 22.7 us  [first_products(): pl.pallas_call(lambda *refs: first_kernel(norm_factor, *refs), grid_spec=...]
  transfers between devices with their start and end apart: 2 -> 7, of which waited for: 2 -> 4; matrix products, arithmetic and copies ran while one was open for 1% -> 2% of each run, Pallas kernels for 0% -> 7%
where the time goes in v2:
time: 317 us; the launch traced here: 315 us
  waiting for transfers between devices  186 us (59%)
  blocking collectives  49.4 us (16%)
  Pallas kernels  38.2 us (12%)
  starting transfers between devices  14.6 us (5%)
  between operations  13.7 us (4%)
  other arithmetic  7.39 us (2%)
  local copies, waits for them, and re-layouts  5.22 us (2%)
    ppermute x2, waiting for transfers between devices, body(): came = lax.ppermute(node_blocks, 'ops', crossing)  99.7 us
    all_gather x1, waiting for transfers between devices, body(): far_rows = lax.all_gather(far_nodes, 'tm', axis=0, tiled=True)  69.9 us
    all_to_all x1, blocking collectives, body(): lax.all_to_all(partial_sum, 'ops', split_axis=0, concat_axis=0, tiled=True)  49.4 us
    pallas_call x5, Pallas kernels, first_products(): pl.pallas_call(lambda *refs: first_kernel(norm_factor, *refs), grid_spec=...  22.7 us
    ppermute x3, waiting for transfers between devices, body(): regions[turn] = lax.ppermute(near_products(turn), 'ops', pairs)  15.6 us
    pallas_call x1, Pallas kernels, second_sums(): pl.pallas_call(lambda *refs: second_kernel(len(regions), norm_factor, *re...  15.5 us
    ppermute x2, starting transfers between devices, body(): came = lax.ppermute(node_blocks, 'ops', crossing)  9.35 us
  transfers between devices with their start and end apart: 7, of which 4 were waited for; matrix products, arithmetic and copies ran while one was open for 2% of the time, Pallas kernels for 7%

profile of v2, /device:TPU:0, one launch (start us, length us, event | category | flops | bytes accessed | tf_op | source)
XLA Modules:
  0.0 314.7 jit_solution(5862606879043034712)
XLA Ops:
  6.5 0.7 all-gather.3.cloned.1.call-update
  7.3 6.1 %collective-permute-start.4 = (bf16[4,384,768]{2,1,0:T(8,128)(2,1)}, bf16[4,384,768]{2,1,0:T(8,128)(2,1)S(1)}, u32[]{:S(2)}, u32[]{:S(2)}) collective-permute-start(bf16[4,384,768]{2,1,0:T(8,128)(2,1)} %param.11), channel_id=1, source_target_pairs={{0,2},{3,1},{4,6},{7,5},{8,10},{11,9},{12,14},{15,13},{16,18},{19,... | collective-permute-start | bytes 7077896 | tf_op jit(solution)/shard_map/ppermute | solution.py:152
  13.4 3.3 %collective-permute-start.3 = (bf16[4,384,768]{2,1,0:T(8,128)(2,1)}, bf16[4,384,768]{2,1,0:T(8,128)(2,1)}, u32[]{:S(2)}, u32[]{:S(2)}) collective-permute-start(bf16[4,384,768]{2,1,0:T(8,128)(2,1)} %param.11), channel_id=1, source_target_pairs={{0,3},{3,0},{4,7},{7,4},{8,11},{11,8},{12,15},{15,12},{16,19},{19,... | collective-permute-start | bytes 7077896 | tf_op jit(solution)/shard_map/ppermute | solution.py:152
  16.7 48.5 %collective-permute-done.4 = bf16[4,384,768]{2,1,0:T(8,128)(2,1)S(1)} collective-permute-done((bf16[4,384,768]{2,1,0:T(8,128)(2,1)}, bf16[4,384,768]{2,1,0:T(8,128)(2,1)S(1)}, u32[]{:S(2)}, u32[]{:S(2)}) %collective-permute-start.4) | collective-permute-done | bytes 2359328 | tf_op jit(solution)/shard_map/ppermute | solution.py:152
  65.2 51.2 %collective-permute-done.3 = bf16[4,384,768]{2,1,0:T(8,128)(2,1)} collective-permute-done((bf16[4,384,768]{2,1,0:T(8,128)(2,1)}, bf16[4,384,768]{2,1,0:T(8,128)(2,1)}, u32[]{:S(2)}, u32[]{:S(2)}) %collective-permute-start.3) | collective-permute-done | bytes 2359328 | tf_op jit(solution)/shard_map/ppermute | solution.py:152
  116.4 3.5 %broadcast_select_fusion = bf16[4,384,768]{2,1,0:T(8,128)(2,1)} fusion(bf16[4,384,768]{2,1,0:T(8,128)(2,1)} %collective-permute-done.3, bf16[4,384,768]{2,1,0:T(8,128)(2,1)S(1)} %collective-permute-done.4, pred[]{:T(512)S(6)} %or.7), kind=kLoop, calls=%fused_computation.1 | loop fusion | flops 1179648 | bytes 7077889 | tf_op jit(solution)/shard_map/jit(_where)/select_n | solution.py:154
  120.0 0.6 copy-done.12
  122.7 0.3 select_reduce_fusion
  123.1 3.4 %first_section.6 = bf16[4,384,768]{2,1,0:T(8,128)(2,1)S(1)} custom-call(s32[4]{0:T(128)S(1)} %get-tuple-element.33.refs_0_, s32[4]{0:T(128)S(1)} %get-tuple-element.29.refs_1_, s32[4]{0:T(128)S(1)} %get-tuple-element.25.refs_2_, bf16[32,384,768]{2,1,0:T(8,128)(2,1)} %all-gather.3.cloned.1.call-done.refs_3_.refs_4_, ...), custom_call_target="tpu_custom_call" | custom-call | flops 1811939328 | bytes 7077888 | tf_op jit(solution)/shard_map/first_section/pallas_call | solution.py:64
  126.6 2.7 collective-permute-start
  129.2 5.1 %first_section.7 = bf16[4,384,768]{2,1,0:T(8,128)(2,1)} custom-call(s32[4]{0:T(128)S(1)} %get-tuple-element.32.refs_0_, s32[4]{0:T(128)S(1)} %get-tuple-element.28.refs_1_, s32[4]{0:T(128)S(1)} %get-tuple-element.24.refs_2_, bf16[32,384,768]{2,1,0:T(8,128)(2,1)} %all-gather.3.cloned.1.call-done.refs_3_.refs_4_, ...), custom_call_target="tpu_custom_call" | custom-call | flops 1811939328 | bytes 7077888 | tf_op jit(solution)/shard_map/first_section/pallas_call | solution.py:64
  134.3 1.3 collective-permute-start.1
  135.6 4.7 %first_section.8 = bf16[4,384,768]{2,1,0:T(8,128)(2,1)} custom-call(s32[4]{0:T(128)S(1)} %get-tuple-element.31.refs_0_, s32[4]{0:T(128)S(1)} %get-tuple-element.27.refs_1_, s32[4]{0:T(128)S(1)} %get-tuple-element.23.refs_2_, bf16[32,384,768]{2,1,0:T(8,128)(2,1)} %all-gather.3.cloned.1.call-done.refs_3_.refs_4_, ...), custom_call_target="tpu_custom_call" | custom-call | flops 1811939328 | bytes 7077888 | tf_op jit(solution)/shard_map/first_section/pallas_call | solution.py:64
  140.3 1.3 collective-permute-start.2
  141.6 0.6 dynamic_slice.77.refs_4_
  143.5 4.2 %first_section.5.refs_5_ = bf16[4,384,768]{2,1,0:T(8,128)(2,1)S(1)} custom-call(s32[4]{0:T(128)S(1)} %get-tuple-element.34.refs_0_, s32[4]{0:T(128)S(1)} %get-tuple-element.30.refs_1_, s32[4]{0:T(128)S(1)} %get-tuple-element.26.refs_2_, bf16[32,384,768]{2,1,0:T(8,128)(2,1)} %all-gather.3.cloned.1.call-done.refs_3_.refs_4_, ...), custom_call_target="tpu_custom_call" | custom-call | flops 1811939328 | bytes 7077888 | tf_op jit(solution)/shard_map/first_section/pallas_call | solution.py:64
  147.7 1.4 copy-done.2
  149.1 69.9 %all-gather.5.cloned.1.call-done.refs_3_.refs_4_ = bf16[32,384,768]{2,1,0:T(8,128)(2,1)} async-done(((bf16[4,384,768]{2,1,0:T(8,128)(2,1)}), bf16[32,384,768]{2,1,0:T(8,128)(2,1)}) %all-gather.5.cloned.1.call-update) | async-done | bytes 18874384 | tf_op jit(solution)/shard_map/all_gather | solution.py:155
  219.1 5.3 %first_section.9.refs_9_ = bf16[4,384,768]{2,1,0:T(8,128)(2,1)S(1)} custom-call(s32[4]{0:T(128)S(1)} %get-tuple-element.14.refs_0_, s32[4]{0:T(128)S(1)} %get-tuple-element.13.refs_1_, s32[4]{0:T(128)S(1)} %convert_element_type.18.refs_2_, bf16[32,384,768]{2,1,0:T(8,128)(2,1)} %all-gather.5.cloned.1.call-done.refs_3_.refs_4_, ...), custom_call_target="tpu_custom_call" | custom-call | flops 1811939328 | bytes 7077888 | tf_op jit(solution)/shard_map/first_section/pallas_call | solution.py:64
  224.4 1.5 copy-done.4
  225.9 15.6 %collective-permute-done.2.refs_8_ = bf16[4,384,768]{2,1,0:T(8,128)(2,1)} collective-permute-done((bf16[4,384,768]{2,1,0:T(8,128)(2,1)}, bf16[4,384,768]{2,1,0:T(8,128)(2,1)}, u32[]{:S(2)}, u32[]{:S(2)}) %collective-permute-start.2) | collective-permute-done | bytes 2359328 | tf_op jit(solution)/shard_map/ppermute | solution.py:231
  241.5 15.5 %second_section.1 = bf16[4,384,768]{2,1,0:T(8,128)(2,1)S(1)} custom-call(s32[16]{0:T(128)S(1)} %get-tuple-element.20.refs_0_, s32[16]{0:T(128)S(1)} %get-tuple-element.19.refs_1_, s32[16]{0:T(128)S(1)} %get-tuple-element.44.refs_2_, s32[16]{0:T(128)S(1)} %get-tuple-element.43.refs_3_, s32[1]{0:T(128)} %dynamic_slice.77.refs_4_, ...), custom_call_target="tpu_custom_call" | custom-call | flops 7247757312 | bytes 28311552 | tf_op jit(solution)/shard_map/second_section/pallas_call | solution.py:87
  257.0 49.4 %all_to_all.5 = bf16[4,384,768]{2,1,0:T(8,128)(2,1)S(1)} all-to-all(bf16[4,384,768]{2,1,0:T(8,128)(2,1)S(1)} %second_section.1), channel_id=1, replica_groups=mesh['tm'=8,'ops'=4] {'ops'}, dimensions={0} | all-to-all | bytes 4718592 | tf_op jit(solution)/shard_map/all_to_all | solution.py:247
  306.5 1.3 convert_reduce_fusion
  (69 shorter events, 3.5 us)
Async XLA Ops:
  6.5 114.2 %copy-start = (s32[32,16]{0,1:T(8,128)S(1)}, s32[32,16]{0,1:T(8,128)}, u32[]{:S(2)}) copy-start(s32[32,16]{0,1:T(8,128)} %param.15) | copy-start | bytes 6148
  6.5 116.6 %all-gather.3.cloned.1.call-start = ((), (), s32[]{:S(2)}) async-start(), calls=%async_computation.1 | async-start | bytes 21233664 | tf_op jit(solution)/shard_map/all_gather | solution.py:148
  7.3 211.8 %all-gather.5.cloned.1.call-start = ((), (), s32[]{:S(2)}) async-start(), calls=%async_computation.2 | async-start | bytes 21233664 | tf_op jit(solution)/shard_map/all_gather | solution.py:155
  7.3 57.9 %collective-permute-start.4 = (bf16[4,384,768]{2,1,0:T(8,128)(2,1)}, bf16[4,384,768]{2,1,0:T(8,128)(2,1)S(1)}, u32[]{:S(2)}, u32[]{:S(2)}) collective-permute-start(bf16[4,384,768]{2,1,0:T(8,128)(2,1)} %param.11), channel_id=1, source_target_pairs={{0,2},{3,1},{4,6},{7,5},{8,10},{11,9},{12,14},{15,13},{16,18},{19,... | collective-permute-start | bytes 7077896 | tf_op jit(solution)/shard_map/ppermute | solution.py:152
  13.4 103.0 %collective-permute-start.3 = (bf16[4,384,768]{2,1,0:T(8,128)(2,1)}, bf16[4,384,768]{2,1,0:T(8,128)(2,1)}, u32[]{:S(2)}, u32[]{:S(2)}) collective-permute-start(bf16[4,384,768]{2,1,0:T(8,128)(2,1)} %param.11), channel_id=1, source_target_pairs={{0,3},{3,0},{4,7},{7,4},{8,11},{11,8},{12,15},{15,12},{16,19},{19,... | collective-permute-start | bytes 7077896 | tf_op jit(solution)/shard_map/ppermute | solution.py:152
  120.0 0.7 copy-start.12
  120.0 0.9 copy-start.8
  120.0 0.9 copy-start.9
  120.0 1.1 copy-start.7
  120.0 1.3 copy-start.5
  120.0 1.3 copy-start.6
  126.6 99.3 %collective-permute-start = (bf16[4,384,768]{2,1,0:T(8,128)(2,1)S(1)}, bf16[4,384,768]{2,1,0:T(8,128)(2,1)}, u32[]{:S(2)}, u32[]{:S(2)}) collective-permute-start(bf16[4,384,768]{2,1,0:T(8,128)(2,1)S(1)} %first_section.6), channel_id=1, source_target_pairs={{0,1},{1,2},{2,3},{4,5},{5,6},{6,7},{8,9},{9,10},{10,11},{12,13},{... | collective-permute-start | bytes 7077896 | tf_op jit(solution)/shard_map/ppermute | solution.py:231
  134.3 91.5 %collective-permute-start.1 = (bf16[4,384,768]{2,1,0:T(8,128)(2,1)}, bf16[4,384,768]{2,1,0:T(8,128)(2,1)}, u32[]{:S(2)}, u32[]{:S(2)}) collective-permute-start(bf16[4,384,768]{2,1,0:T(8,128)(2,1)} %first_section.7), channel_id=1, source_target_pairs={{1,3},{2,0},{5,7},{6,4},{9,11},{10,8},{13,15},{14,12},{17,19},{18,... | collective-permute-start | bytes 7077896 | tf_op jit(solution)/shard_map/ppermute | solution.py:231
  135.6 6.9 %copy-start.10 = (s32[32,16]{0,1:T(8,128)S(1)}, s32[32,16]{0,1:T(8,128)}, u32[]{:S(2)}) copy-start(s32[32,16]{0,1:T(8,128)} %param.20) | copy-start | bytes 6148
  135.6 6.9 %copy-start.11 = (s32[32,16]{0,1:T(8,128)S(1)}, s32[32,16]{0,1:T(8,128)}, u32[]{:S(2)}) copy-start(s32[32,16]{0,1:T(8,128)} %param.19) | copy-start | bytes 6148
  140.3 101.2 %collective-permute-start.2 = (bf16[4,384,768]{2,1,0:T(8,128)(2,1)}, bf16[4,384,768]{2,1,0:T(8,128)(2,1)}, u32[]{:S(2)}, u32[]{:S(2)}) collective-permute-start(bf16[4,384,768]{2,1,0:T(8,128)(2,1)} %first_section.8), channel_id=1, source_target_pairs={{1,0},{2,1},{3,2},{5,4},{6,5},{7,6},{9,8},{10,9},{11,10},{13,12},{... | collective-permute-start | bytes 7077896 | tf_op jit(solution)/shard_map/ppermute | solution.py:231
  147.7 1.4 copy-start.2
  219.0 22.5 %copy-start.3 = (bf16[4,384,768]{2,1,0:T(8,128)(2,1)S(1)}, bf16[4,384,768]{2,1,0:T(8,128)(2,1)}, u32[]{:S(2)}) copy-start(bf16[4,384,768]{2,1,0:T(8,128)(2,1)} %copy-done.2) | copy-start | bytes 7077892
  224.4 1.5 copy-start.4
  257.0 50.8 %copy-start.1 = (s32[32,16]{0,1:T(8,128)S(1)}, s32[32,16]{0,1:T(8,128)}, u32[]{:S(2)}) copy-start(s32[32,16]{0,1:T(8,128)} %param.15) | copy-start | bytes 6148
Sparse Core Ops, SparseCore 0:
  9.2 101.4 all-gather.2
  120.1 98.8 all-gather.4

commit v3 on v2

--- a/solution.py
+++ b/solution.py
@@ -146,12 +146,25 @@
 
     far_index = jnp.where(group_index >= half, 0, group_count - 1)
     near_rows = lax.all_gather(node_blocks, "tm", axis=0, tiled=True)
-    far_nodes = None
-    for step in range(half):
-        crossing = [(0, half + step), (group_count - 1, half - 1 - step)]
-        came = lax.ppermute(node_blocks, "ops", crossing)
-        takes = jnp.logical_or(group_index == half + step, group_index == half - 1 - step)
-        far_nodes = came if far_nodes is None else jnp.where(takes, came, far_nodes)
+    cuts = 2 if held_nodes % 2 == 0 else 1
+    pieces = jnp.split(node_blocks, cuts, axis=0)
+    chains = [[] for _ in range(cuts)]
+    for cut in range(cuts):
+        came = lax.ppermute(pieces[cut], "ops", [(0, half), (group_count - 1, half - 1)])
+        chains[cut].append(came)
+    for step in range(1, half):
+        onward = [(half + step - 1, half + step), (half - step, half - 1 - step)]
+        for cut in range(cuts):
+            chains[cut].append(lax.ppermute(chains[cut][-1], "ops", onward))
+    hop = jnp.where(group_index >= half, group_index - half, half - 1 - group_index)
+
+    def arrived_at(chain):
+        block = chain[0]
+        for step in range(1, half):
+            block = jnp.where(hop == step, chain[step], block)
+        return block
+
+    far_nodes = jnp.concatenate([arrived_at(chain) for chain in chains], axis=0)
     far_rows = lax.all_gather(far_nodes, "tm", axis=0, tiled=True)
 
     def own_rows(table):

time: 317 us -> 308 us (0.972)
  the two profiles are of different devices: /device:TPU:0 before, /device:TPU:4 now
where the time goes in v3:
time: 308 us; the launch traced here: 306 us
  waiting for transfers between devices  172 us (56%)
  blocking collectives  62.6 us (20%)
  Pallas kernels  28.8 us (9%)
  starting transfers between devices  15.5 us (5%)
  between operations  13.7 us (4%)
  other arithmetic  6.98 us (2%)
  local copies, waits for them, and re-layouts  6.18 us (2%)
    all_gather x1, waiting for transfers between devices, body(): far_rows = lax.all_gather(far_nodes, 'tm', axis=0, tiled=True)  72.1 us
    all_to_all x1, blocking collectives, body(): lax.all_to_all(partial_sum, 'ops', split_axis=0, concat_axis=0, tiled=True)  62.6 us
    ppermute x2, waiting for transfers between devices, body(): lax.ppermute(pieces[cut], 'ops', [(0, half), (group_count - 1, half - 1)])  47.8 us
    ppermute x2, waiting for transfers between devices, body(): chains[cut].append(lax.ppermute(chains[cut][-1], 'ops', onward))  27.4 us
    pallas_call x5, Pallas kernels, first_products(): pl.pallas_call(lambda *refs: first_kernel(norm_factor, *refs), grid_spec=...  22.1 us
    ppermute x3, waiting for transfers between devices, body(): regions[turn] = lax.ppermute(near_products(turn), 'ops', pairs)  13.8 us
    all_gather x1, waiting for transfers between devices, body(): near_rows = lax.all_gather(node_blocks, 'tm', axis=0, tiled=True)  10 us
    ppermute x3, starting transfers between devices, body(): regions[turn] = lax.ppermute(near_products(turn), 'ops', pairs)  7 us
  transfers between devices with their start and end apart: 9, of which 7 were waited for; matrix products, arithmetic and copies ran while one was open for 2% of the time, Pallas kernels for 7%

profile of v3, /device:TPU:4, one launch (start us, length us, event | category | flops | bytes accessed | tf_op | source)
XLA Modules:
  0.0 305.7 jit_solution(9172209999556707971)
XLA Ops:
  8.4 4.6 %collective-permute-start.3 = (bf16[2,384,768]{2,1,0:T(8,128)(2,1)S(1)}, bf16[2,384,768]{2,1,0:T(8,128)(2,1)S(1)}, u32[]{:S(2)}, u32[]{:S(2)}) collective-permute-start(bf16[2,384,768]{2,1,0:T(8,128)(2,1)S(1)} %get-tuple-element.21), channel_id=1, source_target_pairs={{0,2},{3,1},{4,6},{7,5},{8,10},{11,9},{12,14},{15,13},{16,18},{19,... | collective-permute-start | bytes 3538952 | tf_op jit(solution)/shard_map/ppermute | solution.py:153
  12.9 1.4 collective-permute-start.5
  14.3 24.9 %collective-permute-done.3 = bf16[2,384,768]{2,1,0:T(8,128)(2,1)S(1)} collective-permute-done((bf16[2,384,768]{2,1,0:T(8,128)(2,1)S(1)}, bf16[2,384,768]{2,1,0:T(8,128)(2,1)S(1)}, u32[]{:S(2)}, u32[]{:S(2)}) %collective-permute-start.3) | collective-permute-done | bytes 1179680 | tf_op jit(solution)/shard_map/ppermute | solution.py:153
  39.2 1.3 collective-permute-start.4
  40.5 22.8 %collective-permute-done.5 = bf16[2,384,768]{2,1,0:T(8,128)(2,1)S(1)} collective-permute-done((bf16[2,384,768]{2,1,0:T(8,128)(2,1)S(1)}, bf16[2,384,768]{2,1,0:T(8,128)(2,1)S(1)}, u32[]{:S(2)}, u32[]{:S(2)}) %collective-permute-start.5) | collective-permute-done | bytes 1179680 | tf_op jit(solution)/shard_map/ppermute | solution.py:153
  63.4 1.3 collective-permute-start.6
  64.7 2.1 collective-permute-done.4
  66.9 25.3 %collective-permute-done.6 = bf16[2,384,768]{2,1,0:T(8,128)(2,1)} collective-permute-done((bf16[2,384,768]{2,1,0:T(8,128)(2,1)S(1)}, bf16[2,384,768]{2,1,0:T(8,128)(2,1)}, u32[]{:S(2)}, u32[]{:S(2)}) %collective-permute-start.6) | collective-permute-done | bytes 1179680 | tf_op jit(solution)/shard_map/ppermute | solution.py:158
  92.2 1.4 broadcast_select_fusion
  93.6 1.6 pad_maximum_fusion
  98.4 10.0 %all-gather.3.cloned.1.call-done.refs_3_.refs_4_ = bf16[32,384,768]{2,1,0:T(8,128)(2,1)} async-done(((bf16[4,384,768]{2,1,0:T(8,128)(2,1)}), bf16[32,384,768]{2,1,0:T(8,128)(2,1)}) %all-gather.3.cloned.1.call-update) | async-done | bytes 18874384 | tf_op jit(solution)/shard_map/all_gather | solution.py:148
  108.4 4.8 %first_section.6 = bf16[4,384,768]{2,1,0:T(8,128)(2,1)S(1)} custom-call(s32[4]{0:T(128)S(1)} %get-tuple-element.35.refs_0_, s32[4]{0:T(128)S(1)} %get-tuple-element.31.refs_1_, s32[4]{0:T(128)S(1)} %get-tuple-element.27.refs_2_, bf16[32,384,768]{2,1,0:T(8,128)(2,1)} %all-gather.3.cloned.1.call-done.refs_3_.refs_4_, ...), custom_call_target="tpu_custom_call" | custom-call | flops 1811939328 | bytes 7077888 | tf_op jit(solution)/shard_map/first_section/pallas_call | solution.py:64
  113.2 4.4 %collective-permute-start = (bf16[4,384,768]{2,1,0:T(8,128)(2,1)S(1)}, bf16[4,384,768]{2,1,0:T(8,128)(2,1)}, u32[]{:S(2)}, u32[]{:S(2)}) collective-permute-start(bf16[4,384,768]{2,1,0:T(8,128)(2,1)S(1)} %first_section.6), channel_id=1, source_target_pairs={{0,1},{1,2},{2,3},{4,5},{5,6},{6,7},{8,9},{9,10},{10,11},{12,13},{... | collective-permute-start | bytes 7077896 | tf_op jit(solution)/shard_map/ppermute | solution.py:244
  117.6 5.1 %first_section.7 = bf16[4,384,768]{2,1,0:T(8,128)(2,1)} custom-call(s32[4]{0:T(128)S(1)} %get-tuple-element.34.refs_0_, s32[4]{0:T(128)S(1)} %get-tuple-element.30.refs_1_, s32[4]{0:T(128)S(1)} %get-tuple-element.26.refs_2_, bf16[32,384,768]{2,1,0:T(8,128)(2,1)} %all-gather.3.cloned.1.call-done.refs_3_.refs_4_, ...), custom_call_target="tpu_custom_call" | custom-call | flops 1811939328 | bytes 7077888 | tf_op jit(solution)/shard_map/first_section/pallas_call | solution.py:64
  124.0 4.8 %first_section.8 = bf16[4,384,768]{2,1,0:T(8,128)(2,1)} custom-call(s32[4]{0:T(128)S(1)} %get-tuple-element.33.refs_0_, s32[4]{0:T(128)S(1)} %get-tuple-element.29.refs_1_, s32[4]{0:T(128)S(1)} %get-tuple-element.25.refs_2_, bf16[32,384,768]{2,1,0:T(8,128)(2,1)} %all-gather.3.cloned.1.call-done.refs_3_.refs_4_, ...), custom_call_target="tpu_custom_call" | custom-call | flops 1811939328 | bytes 7077888 | tf_op jit(solution)/shard_map/first_section/pallas_call | solution.py:64
  132.0 3.5 %first_section.5.refs_5_ = bf16[4,384,768]{2,1,0:T(8,128)(2,1)S(1)} custom-call(s32[4]{0:T(128)S(1)} %get-tuple-element.36.refs_0_, s32[4]{0:T(128)S(1)} %get-tuple-element.32.refs_1_, s32[4]{0:T(128)S(1)} %get-tuple-element.28.refs_2_, bf16[32,384,768]{2,1,0:T(8,128)(2,1)} %all-gather.3.cloned.1.call-done.refs_3_.refs_4_, ...), custom_call_target="tpu_custom_call" | custom-call | flops 1811939328 | bytes 7077888 | tf_op jit(solution)/shard_map/first_section/pallas_call | solution.py:64
  135.5 1.4 copy-done.2
  136.9 72.1 %all-gather.5.cloned.1.call-done.refs_3_.refs_4_ = bf16[32,384,768]{2,1,0:T(8,128)(2,1)} async-done(((bf16[4,384,768]{2,1,0:T(8,128)(2,1)}), bf16[32,384,768]{2,1,0:T(8,128)(2,1)}) %all-gather.5.cloned.1.call-update) | async-done | bytes 18874384 | tf_op jit(solution)/shard_map/all_gather | solution.py:168
  209.0 3.9 %first_section.9.refs_9_ = bf16[4,384,768]{2,1,0:T(8,128)(2,1)S(1)} custom-call(s32[4]{0:T(128)S(1)} %get-tuple-element.14.refs_0_, s32[4]{0:T(128)S(1)} %get-tuple-element.13.refs_1_, s32[4]{0:T(128)S(1)} %convert_element_type.18.refs_2_, bf16[32,384,768]{2,1,0:T(8,128)(2,1)} %all-gather.5.cloned.1.call-done.refs_3_.refs_4_, ...), custom_call_target="tpu_custom_call" | custom-call | flops 1811939328 | bytes 7077888 | tf_op jit(solution)/shard_map/first_section/pallas_call | solution.py:64
  213.0 1.4 copy-done.4
  214.3 13.8 %collective-permute-done.2.refs_8_ = bf16[4,384,768]{2,1,0:T(8,128)(2,1)} collective-permute-done((bf16[4,384,768]{2,1,0:T(8,128)(2,1)}, bf16[4,384,768]{2,1,0:T(8,128)(2,1)}, u32[]{:S(2)}, u32[]{:S(2)}) %collective-permute-start.2) | collective-permute-done | bytes 2359328 | tf_op jit(solution)/shard_map/ppermute | solution.py:244
  228.2 6.7 %second_section.1 = bf16[4,384,768]{2,1,0:T(8,128)(2,1)S(1)} custom-call(s32[16]{0:T(128)S(1)} %get-tuple-element.20.refs_0_, s32[16]{0:T(128)S(1)} %get-tuple-element.19.refs_1_, s32[16]{0:T(128)S(1)} %get-tuple-element.46.refs_2_, s32[16]{0:T(128)S(1)} %get-tuple-element.45.refs_3_, s32[1]{0:T(128)} %dynamic_slice.77.refs_4_, ...), custom_call_target="tpu_custom_call" | custom-call | flops 7247757312 | bytes 28311552 | tf_op jit(solution)/shard_map/second_section/pallas_call | solution.py:87
  234.9 62.6 %all_to_all.5 = bf16[4,384,768]{2,1,0:T(8,128)(2,1)S(1)} all-to-all(bf16[4,384,768]{2,1,0:T(8,128)(2,1)S(1)} %second_section.1), channel_id=1, replica_groups=mesh['tm'=8,'ops'=4] {'ops'}, dimensions={0} | all-to-all | bytes 4718592 | tf_op jit(solution)/shard_map/all_to_all | solution.py:260
  297.5 1.3 convert_reduce_fusion
  (78 shorter events, 9.4 us)
Async XLA Ops:
  6.5 89.4 %copy-start = (s32[32,16]{0,1:T(8,128)S(1)}, s32[32,16]{0,1:T(8,128)}, u32[]{:S(2)}) copy-start(s32[32,16]{0,1:T(8,128)} %param.15) | copy-start | bytes 6148
  6.5 1.7 copy-start.5
  6.5 101.8 %all-gather.3.cloned.1.call-start = ((), (), s32[]{:S(2)}) async-start(), calls=%async_computation.1 | async-start | bytes 21233664 | tf_op jit(solution)/shard_map/all_gather | solution.py:148
  7.3 201.8 %all-gather.5.cloned.1.call-start = ((), (), s32[]{:S(2)}) async-start(), calls=%async_computation.2 | async-start | bytes 21233664 | tf_op jit(solution)/shard_map/all_gather | solution.py:168
  8.4 30.9 %collective-permute-start.3 = (bf16[2,384,768]{2,1,0:T(8,128)(2,1)S(1)}, bf16[2,384,768]{2,1,0:T(8,128)(2,1)S(1)}, u32[]{:S(2)}, u32[]{:S(2)}) collective-permute-start(bf16[2,384,768]{2,1,0:T(8,128)(2,1)S(1)} %get-tuple-element.21), channel_id=1, source_target_pairs={{0,2},{3,1},{4,6},{7,5},{8,10},{11,9},{12,14},{15,13},{16,18},{19,... | collective-permute-start | bytes 3538952 | tf_op jit(solution)/shard_map/ppermute | solution.py:153
  12.9 50.4 %collective-permute-start.5 = (bf16[2,384,768]{2,1,0:T(8,128)(2,1)S(1)}, bf16[2,384,768]{2,1,0:T(8,128)(2,1)S(1)}, u32[]{:S(2)}, u32[]{:S(2)}) collective-permute-start(bf16[2,384,768]{2,1,0:T(8,128)(2,1)S(1)} %get-tuple-element.22), channel_id=1, source_target_pairs={{0,2},{3,1},{4,6},{7,5},{8,10},{11,9},{12,14},{15,13},{16,18},{19,... | collective-permute-start | bytes 3538952 | tf_op jit(solution)/shard_map/ppermute | solution.py:153
  39.2 27.6 %collective-permute-start.4 = (bf16[2,384,768]{2,1,0:T(8,128)(2,1)S(1)}, bf16[2,384,768]{2,1,0:T(8,128)(2,1)S(1)}, u32[]{:S(2)}, u32[]{:S(2)}) collective-permute-start(bf16[2,384,768]{2,1,0:T(8,128)(2,1)S(1)} %collective-permute-done.3), channel_id=1, source_target_pairs={{2,3},{1,0},{6,7},{5,4},{10,11},{9,8},{14,15},{13,12},{18,19},{17,... | collective-permute-start | bytes 3538952 | tf_op jit(solution)/shard_map/ppermute | solution.py:158
  63.4 28.8 %collective-permute-start.6 = (bf16[2,384,768]{2,1,0:T(8,128)(2,1)S(1)}, bf16[2,384,768]{2,1,0:T(8,128)(2,1)}, u32[]{:S(2)}, u32[]{:S(2)}) collective-permute-start(bf16[2,384,768]{2,1,0:T(8,128)(2,1)S(1)} %collective-permute-done.5), channel_id=1, source_target_pairs={{2,3},{1,0},{6,7},{5,4},{10,11},{9,8},{14,15},{13,12},{18,19},{17,... | collective-permute-start | bytes 3538952 | tf_op jit(solution)/shard_map/ppermute | solution.py:158
  95.2 0.7 copy-start.13
  95.2 0.9 copy-start.9
  95.2 0.9 copy-start.10
  95.2 1.1 copy-start.8
  95.2 1.3 copy-start.6
  95.2 1.3 copy-start.7
  113.2 101.2 %collective-permute-start = (bf16[4,384,768]{2,1,0:T(8,128)(2,1)S(1)}, bf16[4,384,768]{2,1,0:T(8,128)(2,1)}, u32[]{:S(2)}, u32[]{:S(2)}) collective-permute-start(bf16[4,384,768]{2,1,0:T(8,128)(2,1)S(1)} %first_section.6), channel_id=1, source_target_pairs={{0,1},{1,2},{2,3},{4,5},{5,6},{6,7},{8,9},{9,10},{10,11},{12,13},{... | collective-permute-start | bytes 7077896 | tf_op jit(solution)/shard_map/ppermute | solution.py:244
  122.7 91.6 %collective-permute-start.1 = (bf16[4,384,768]{2,1,0:T(8,128)(2,1)}, bf16[4,384,768]{2,1,0:T(8,128)(2,1)}, u32[]{:S(2)}, u32[]{:S(2)}) collective-permute-start(bf16[4,384,768]{2,1,0:T(8,128)(2,1)} %first_section.7), channel_id=1, source_target_pairs={{1,3},{2,0},{5,7},{6,4},{9,11},{10,8},{13,15},{14,12},{17,19},{18,... | collective-permute-start | bytes 7077896 | tf_op jit(solution)/shard_map/ppermute | solution.py:244
  124.0 7.1 %copy-start.11 = (s32[32,16]{0,1:T(8,128)S(1)}, s32[32,16]{0,1:T(8,128)}, u32[]{:S(2)}) copy-start(s32[32,16]{0,1:T(8,128)} %param.20) | copy-start | bytes 6148
  124.0 7.1 %copy-start.12 = (s32[32,16]{0,1:T(8,128)S(1)}, s32[32,16]{0,1:T(8,128)}, u32[]{:S(2)}) copy-start(s32[32,16]{0,1:T(8,128)} %param.19) | copy-start | bytes 6148
  128.9 99.3 %collective-permute-start.2 = (bf16[4,384,768]{2,1,0:T(8,128)(2,1)}, bf16[4,384,768]{2,1,0:T(8,128)(2,1)}, u32[]{:S(2)}, u32[]{:S(2)}) collective-permute-start(bf16[4,384,768]{2,1,0:T(8,128)(2,1)} %first_section.8), channel_id=1, source_target_pairs={{1,0},{2,1},{3,2},{5,4},{6,5},{7,6},{9,8},{10,9},{11,10},{13,12},{... | collective-permute-start | bytes 7077896 | tf_op jit(solution)/shard_map/ppermute | solution.py:244
  135.5 1.4 copy-start.2
  209.0 19.1 %copy-start.3 = (bf16[4,384,768]{2,1,0:T(8,128)(2,1)S(1)}, bf16[4,384,768]{2,1,0:T(8,128)(2,1)}, u32[]{:S(2)}) copy-start(bf16[4,384,768]{2,1,0:T(8,128)(2,1)} %copy-done.2) | copy-start | bytes 7077892
  212.9 1.4 copy-start.4
  234.9 63.9 %copy-start.1 = (s32[32,16]{0,1:T(8,128)S(1)}, s32[32,16]{0,1:T(8,128)}, u32[]{:S(2)}) copy-start(s32[32,16]{0,1:T(8,128)} %param.15) | copy-start | bytes 6148
Sparse Core Ops, SparseCore 0:
  9.2 99.0 all-gather.2
  110.3 98.7 all-gather.4

commit v4 on v3

--- a/solution.py
+++ b/solution.py
@@ -28,7 +28,7 @@
 
 def second_kernel(region_count, norm, left, right, target, sign, live, *refs):
     regions = refs[:region_count]
-    out_ref, held, total, stacked, arrivals = refs[region_count:]
+    *out_refs, held, total, stacked, arrivals = refs[region_count:]
     slots = regions[0].shape[0]
     copies = [
         pltpu.make_async_copy(regions[k], held.at[pl.ds(k * slots, slots)], arrivals.at[k])
@@ -46,7 +46,9 @@
         product = complex_product(held[left[step]], held[right[step]], stacked)
         total[target[step]] += product * weight
 
-    out_ref[...] = total[...].astype(out_ref.dtype)
+    owned = total.shape[0] // len(out_refs)
+    for k, out_ref in enumerate(out_refs):
+        out_ref[...] = total[pl.ds(k * owned, owned)].astype(out_ref.dtype)
 
 
 def product_cost(count, rank_size):
@@ -80,22 +82,24 @@
     )(left, right, used, blocks, blocks)
 
 
-def second_sums(regions, left, right, target, sign, live, norm_factor, diagram_count):
+def second_sums(regions, left, right, target, sign, live, norm_factor, owner_count):
     steps = left.shape[0]
     slots, rank_size, width = regions[0].shape
-    shape = (diagram_count, rank_size, width)
+    shape = (owner_count * DIAG_DEV, rank_size, width)
+    owned = (DIAG_DEV, rank_size, width)
+    kinds = [jnp.bfloat16] * (owner_count - 1) + [jnp.float32]
     return pl.pallas_call(
         lambda *refs: second_kernel(len(regions), norm_factor, *refs),
         in_specs=[pl.BlockSpec(memory_space=pltpu.SMEM)] * 5
         + [pl.BlockSpec(memory_space=pl.ANY)] * len(regions),
-        out_specs=pl.BlockSpec(memory_space=pltpu.VMEM),
+        out_specs=[pl.BlockSpec(memory_space=pltpu.VMEM)] * owner_count,
         scratch_shapes=[
             pltpu.VMEM((len(regions) * slots, rank_size, width), jnp.bfloat16),
             pltpu.VMEM(shape, jnp.float32),
             pltpu.VMEM((2 * rank_size, width), jnp.bfloat16),
             pltpu.SemaphoreType.DMA((len(regions),)),
         ],
-        out_shape=jax.ShapeDtypeStruct(shape, jnp.bfloat16),
+        out_shape=[jax.ShapeDtypeStruct(owned, kind) for kind in kinds],
         compiler_params=pltpu.CompilerParams(vmem_limit_bytes=VMEM_BYTES),
         cost_estimate=product_cost(steps, rank_size),
         name="second_section",
@@ -226,7 +230,15 @@
     places = (region * second_slots + own_row(ranks))[0]
     second_left_at = pick(places, second_left[worker])
     second_right_at = pick(places, second_right[worker])
-    targets = diagram_ids[worker] - row_start * DIAG_DEV
+    row_targets = diagram_ids[worker] - row_start * DIAG_DEV
+    owners = row_targets // DIAG_DEV
+    mirrored = jnp.where(group_index >= half, group_count - 1 - owners, owners)
+    inner = jnp.where(group_index >= half, group_count - 1 - group_index, group_index)
+    if group_count == 4:
+        owner_place = jnp.where(mirrored >= 2, 3 - mirrored, jnp.where(mirrored == inner, 3, 2))
+    else:
+        owner_place = (owners - group_index - 1 + group_count) % group_count
+    targets = owner_place * DIAG_DEV + row_targets % DIAG_DEV
 
     def near_products(turn):
         return first_products(
@@ -247,7 +259,7 @@
         far_rows, far_left[0], far_right[0], far_used[0], norm_factor
     )
     regions = [regions[0] if block is None else block for block in regions]
-    partial_sum = second_sums(
+    sums = second_sums(
         regions,
         second_left_at,
         second_right_at,
@@ -255,11 +267,29 @@
         diagram_signs[worker],
         second_live[worker][None],
         norm_factor,
-        group_count * DIAG_DEV,
-    )
-    terms = lax.all_to_all(partial_sum, "ops", split_axis=0, concat_axis=0, tiled=True)
-    terms = terms.reshape((group_count, DIAG_DEV) + terms.shape[1:])
-    return jnp.sum(terms.astype(jnp.float32), axis=0)
+        group_count,
+    )
+    result = sums[-1]
+    if group_count == 4:
+        inward = [(0, 1), (3, 2)]
+        end_came = lax.ppermute(sums[0], "ops", inward)
+        inner_came = lax.ppermute(sums[1], "ops", inward)
+        partner = lax.ppermute(sums[2], "ops", [(0, 1), (1, 0), (2, 3), (3, 2)])
+        to_end = sums[0].astype(jnp.float32) + end_came.astype(jnp.float32)
+        to_inner = sums[1].astype(jnp.float32) + inner_came.astype(jnp.float32)
+        at_end = lax.ppermute(to_end.astype(jnp.bfloat16), "ops", [(1, 3), (2, 0)])
+        at_inner = lax.ppermute(to_inner.astype(jnp.bfloat16), "ops", [(1, 2), (2, 1)])
+        came = [partner, at_end, at_inner]
+    else:
+        came = [
+            lax.ppermute(
+                sums[turn - 1], "ops", [(g, (g + turn) % group_count) for g in range(group_count)]
+            )
+            for turn in range(1, group_count)
+        ]
+    for block in came:
+        result = result + block.astype(jnp.float32)
+    return result
 
 
 def solution(mesh):

time: 308 us -> 295 us (0.958)
  the two profiles are of different devices: /device:TPU:4 before, /device:TPU:0 now
where the time goes in v4:
time: 295 us; the launch traced here: 292 us
  waiting for transfers between devices  204 us (69%)
  Pallas kernels  40.3 us (14%)
  starting transfers between devices  20.8 us (7%)
  between operations  13.8 us (5%)
  other arithmetic  7.22 us (2%)
  local copies, waits for them, and re-layouts  6.17 us (2%)
    all_gather x1, waiting for transfers between devices, body(): far_rows = lax.all_gather(far_nodes, 'tm', axis=0, tiled=True)  71.5 us
    ppermute x2, waiting for transfers between devices, body(): lax.ppermute(pieces[cut], 'ops', [(0, half), (group_count - 1, half - 1)])  47.8 us
    ppermute x2, waiting for transfers between devices, body(): chains[cut].append(lax.ppermute(chains[cut][-1], 'ops', onward))  27.4 us
    pallas_call x5, Pallas kernels, first_products(): pl.pallas_call(lambda *refs: first_kernel(norm_factor, *refs), grid_spec=...  24.4 us
    pallas_call x1, Pallas kernels, second_sums(): pl.pallas_call(lambda *refs: second_kernel(len(regions), norm_factor, *re...  15.9 us
    ppermute x3, waiting for transfers between devices, body(): regions[turn] = lax.ppermute(near_products(turn), 'ops', pairs)  14.2 us
    ppermute x1, waiting for transfers between devices, body(): end_came = lax.ppermute(sums[0], 'ops', inward)  12.3 us
    ppermute x1, waiting for transfers between devices, body(): inner_came = lax.ppermute(sums[1], 'ops', inward)  11.2 us
  transfers between devices with their start and end apart: 14, of which 10 were waited for; matrix products, arithmetic and copies ran while one was open for 3% of the time, Pallas kernels for 8%

profile of v4, /device:TPU:0, one launch (start us, length us, event | category | flops | bytes accessed | tf_op | source)
XLA Modules:
  0.0 291.9 jit_solution(1751516865089874313)
XLA Ops:
  8.4 6.0 %collective-permute-start.3 = (bf16[2,384,768]{2,1,0:T(8,128)(2,1)S(1)}, bf16[2,384,768]{2,1,0:T(8,128)(2,1)S(1)}, u32[]{:S(2)}, u32[]{:S(2)}) collective-permute-start(bf16[2,384,768]{2,1,0:T(8,128)(2,1)S(1)} %get-tuple-element.29), channel_id=1, source_target_pairs={{0,2},{3,1},{4,6},{7,5},{8,10},{11,9},{12,14},{15,13},{16,18},{19,... | collective-permute-start | bytes 3538952 | tf_op jit(solution)/shard_map/ppermute | solution.py:157
  14.4 1.4 collective-permute-start.5
  15.8 24.9 %collective-permute-done.3 = bf16[2,384,768]{2,1,0:T(8,128)(2,1)S(1)} collective-permute-done((bf16[2,384,768]{2,1,0:T(8,128)(2,1)S(1)}, bf16[2,384,768]{2,1,0:T(8,128)(2,1)S(1)}, u32[]{:S(2)}, u32[]{:S(2)}) %collective-permute-start.3) | collective-permute-done | bytes 1179680 | tf_op jit(solution)/shard_map/ppermute | solution.py:157
  42.0 22.8 %collective-permute-done.5 = bf16[2,384,768]{2,1,0:T(8,128)(2,1)S(1)} collective-permute-done((bf16[2,384,768]{2,1,0:T(8,128)(2,1)S(1)}, bf16[2,384,768]{2,1,0:T(8,128)(2,1)S(1)}, u32[]{:S(2)}, u32[]{:S(2)}) %collective-permute-start.5) | collective-permute-done | bytes 1179680 | tf_op jit(solution)/shard_map/ppermute | solution.py:157
  66.1 2.1 collective-permute-done.4
  68.4 25.3 %collective-permute-done.6 = bf16[2,384,768]{2,1,0:T(8,128)(2,1)} collective-permute-done((bf16[2,384,768]{2,1,0:T(8,128)(2,1)S(1)}, bf16[2,384,768]{2,1,0:T(8,128)(2,1)}, u32[]{:S(2)}, u32[]{:S(2)}) %collective-permute-start.6) | collective-permute-done | bytes 1179680 | tf_op jit(solution)/shard_map/ppermute | solution.py:162
  93.6 1.4 broadcast_select_fusion
  95.1 1.6 pad_maximum_fusion
  99.8 10.9 %all-gather.3.cloned.1.call-done.refs_3_.refs_4_ = bf16[32,384,768]{2,1,0:T(8,128)(2,1)} async-done(((bf16[4,384,768]{2,1,0:T(8,128)(2,1)}), bf16[32,384,768]{2,1,0:T(8,128)(2,1)}) %all-gather.3.cloned.1.call-update) | async-done | bytes 18874384 | tf_op jit(solution)/shard_map/all_gather | solution.py:152
  110.7 4.5 %first_section.6 = bf16[4,384,768]{2,1,0:T(8,128)(2,1)S(1)} custom-call(s32[4]{0:T(128)S(1)} %get-tuple-element.43.refs_0_, s32[4]{0:T(128)S(1)} %get-tuple-element.39.refs_1_, s32[4]{0:T(128)S(1)} %get-tuple-element.35.refs_2_, bf16[32,384,768]{2,1,0:T(8,128)(2,1)} %all-gather.3.cloned.1.call-done.refs_3_.refs_4_, ...), custom_call_target="tpu_custom_call" | custom-call | flops 1811939328 | bytes 7077888 | tf_op jit(solution)/shard_map/first_section/pallas_call | solution.py:66
  115.2 3.5 %collective-permute-start = (bf16[4,384,768]{2,1,0:T(8,128)(2,1)S(1)}, bf16[4,384,768]{2,1,0:T(8,128)(2,1)}, u32[]{:S(2)}, u32[]{:S(2)}) collective-permute-start(bf16[4,384,768]{2,1,0:T(8,128)(2,1)S(1)} %first_section.6), channel_id=1, source_target_pairs={{0,1},{1,2},{2,3},{4,5},{5,6},{6,7},{8,9},{9,10},{10,11},{12,13},{... | collective-permute-start | bytes 7077896 | tf_op jit(solution)/shard_map/ppermute | solution.py:256
  118.7 5.2 %first_section.7 = bf16[4,384,768]{2,1,0:T(8,128)(2,1)} custom-call(s32[4]{0:T(128)S(1)} %get-tuple-element.42.refs_0_, s32[4]{0:T(128)S(1)} %get-tuple-element.38.refs_1_, s32[4]{0:T(128)S(1)} %get-tuple-element.34.refs_2_, bf16[32,384,768]{2,1,0:T(8,128)(2,1)} %all-gather.3.cloned.1.call-done.refs_3_.refs_4_, ...), custom_call_target="tpu_custom_call" | custom-call | flops 1811939328 | bytes 7077888 | tf_op jit(solution)/shard_map/first_section/pallas_call | solution.py:66
  125.3 4.8 %first_section.8 = bf16[4,384,768]{2,1,0:T(8,128)(2,1)} custom-call(s32[4]{0:T(128)S(1)} %get-tuple-element.41.refs_0_, s32[4]{0:T(128)S(1)} %get-tuple-element.37.refs_1_, s32[4]{0:T(128)S(1)} %get-tuple-element.33.refs_2_, bf16[32,384,768]{2,1,0:T(8,128)(2,1)} %all-gather.3.cloned.1.call-done.refs_3_.refs_4_, ...), custom_call_target="tpu_custom_call" | custom-call | flops 1811939328 | bytes 7077888 | tf_op jit(solution)/shard_map/first_section/pallas_call | solution.py:66
  133.3 5.1 %first_section.5.refs_5_ = bf16[4,384,768]{2,1,0:T(8,128)(2,1)S(1)} custom-call(s32[4]{0:T(128)S(1)} %get-tuple-element.44.refs_0_, s32[4]{0:T(128)S(1)} %get-tuple-element.40.refs_1_, s32[4]{0:T(128)S(1)} %get-tuple-element.36.refs_2_, bf16[32,384,768]{2,1,0:T(8,128)(2,1)} %all-gather.3.cloned.1.call-done.refs_3_.refs_4_, ...), custom_call_target="tpu_custom_call" | custom-call | flops 1811939328 | bytes 7077888 | tf_op jit(solution)/shard_map/first_section/pallas_call | solution.py:66
  138.4 1.4 copy-done.2
  139.8 71.5 %all-gather.5.cloned.1.call-done.refs_3_.refs_4_ = bf16[32,384,768]{2,1,0:T(8,128)(2,1)} async-done(((bf16[4,384,768]{2,1,0:T(8,128)(2,1)}), bf16[32,384,768]{2,1,0:T(8,128)(2,1)}) %all-gather.5.cloned.1.call-update) | async-done | bytes 18874384 | tf_op jit(solution)/shard_map/all_gather | solution.py:172
  211.3 4.6 %first_section.9.refs_9_ = bf16[4,384,768]{2,1,0:T(8,128)(2,1)S(1)} custom-call(s32[4]{0:T(128)S(1)} %get-tuple-element.22.refs_0_, s32[4]{0:T(128)S(1)} %get-tuple-element.21.refs_1_, s32[4]{0:T(128)S(1)} %convert_element_type.41.refs_2_, bf16[32,384,768]{2,1,0:T(8,128)(2,1)} %all-gather.5.cloned.1.call-done.refs_3_.refs_4_, ...), custom_call_target="tpu_custom_call" | custom-call | flops 1811939328 | bytes 7077888 | tf_op jit(solution)/shard_map/first_section/pallas_call | solution.py:66
  216.0 1.4 copy-done.4
  217.4 14.1 %collective-permute-done.2.refs_8_ = bf16[4,384,768]{2,1,0:T(8,128)(2,1)} collective-permute-done((bf16[4,384,768]{2,1,0:T(8,128)(2,1)}, bf16[4,384,768]{2,1,0:T(8,128)(2,1)}, u32[]{:S(2)}, u32[]{:S(2)}) %collective-permute-start.2) | collective-permute-done | bytes 2359328 | tf_op jit(solution)/shard_map/ppermute | solution.py:256
  231.5 15.9 %second_section.1 = (bf16[1,384,768]{2,1,0:T(8,128)(2,1)S(1)}, bf16[1,384,768]{2,1,0:T(8,128)(2,1)S(1)}, bf16[1,384,768]{2,1,0:T(8,128)(2,1)S(1)}, f32[1,384,768]{2,1,0:T(8,128)S(1)}) custom-call(s32[16]{0:T(128)S(1)} %get-tuple-element.28.refs_0_, s32[16]{0:T(128)S(1)} %get-tuple-element.27.refs_1_, s32[16]{0:T(128)S(1)} %compare_select_fusion.6.refs_2_, ...), custom_call_target="tpu_custom_call" | custom-call | flops 7247757312 | bytes 28311552 | tf_op jit(solution)/shard_map/second_section/pallas_call | solution.py:91
  247.5 1.3 collective-permute-start.8
  250.2 12.3 %collective-permute-done.8 = bf16[1,384,768]{2,1,0:T(8,128)(2,1)S(1)} collective-permute-done((bf16[1,384,768]{2,1,0:T(8,128)(2,1)S(1)}, bf16[1,384,768]{2,1,0:T(8,128)(2,1)S(1)}, u32[]{:S(2)}, u32[]{:S(2)}) %collective-permute-start.8) | collective-permute-done | bytes 589856 | tf_op jit(solution)/shard_map/ppermute | solution.py:275
  264.0 11.2 %collective-permute-done.10 = bf16[1,384,768]{2,1,0:T(8,128)(2,1)S(1)} collective-permute-done((bf16[1,384,768]{2,1,0:T(8,128)(2,1)S(1)}, bf16[1,384,768]{2,1,0:T(8,128)(2,1)S(1)}, u32[]{:S(2)}, u32[]{:S(2)}) %collective-permute-start.10) | collective-permute-done | bytes 589856 | tf_op jit(solution)/shard_map/ppermute | solution.py:276
  276.1 7.7 %collective-permute-done.7 = bf16[1,384,768]{2,1,0:T(8,128)(2,1)S(1)} collective-permute-done((bf16[1,384,768]{2,1,0:T(8,128)(2,1)S(1)}, bf16[1,384,768]{2,1,0:T(8,128)(2,1)S(1)}, u32[]{:S(2)}, u32[]{:S(2)}) %collective-permute-start.7) | collective-permute-done | bytes 589856 | tf_op jit(solution)/shard_map/ppermute | solution.py:277
  (90 shorter events, 16.9 us)
Async XLA Ops:
  6.5 90.9 %copy-start = (s32[32,16]{0,1:T(8,128)S(1)}, s32[32,16]{0,1:T(8,128)}, u32[]{:S(2)}) copy-start(s32[32,16]{0,1:T(8,128)} %param.15) | copy-start | bytes 6148
  6.5 1.7 copy-start.5
  6.5 104.2 %all-gather.3.cloned.1.call-start = ((), (), s32[]{:S(2)}) async-start(), calls=%async_computation | async-start | bytes 21233664 | tf_op jit(solution)/shard_map/all_gather | solution.py:152
  7.3 204.1 %all-gather.5.cloned.1.call-start = ((), (), s32[]{:S(2)}) async-start(), calls=%async_computation.1 | async-start | bytes 21233664 | tf_op jit(solution)/shard_map/all_gather | solution.py:172
  8.4 32.3 %collective-permute-start.3 = (bf16[2,384,768]{2,1,0:T(8,128)(2,1)S(1)}, bf16[2,384,768]{2,1,0:T(8,128)(2,1)S(1)}, u32[]{:S(2)}, u32[]{:S(2)}) collective-permute-start(bf16[2,384,768]{2,1,0:T(8,128)(2,1)S(1)} %get-tuple-element.29), channel_id=1, source_target_pairs={{0,2},{3,1},{4,6},{7,5},{8,10},{11,9},{12,14},{15,13},{16,18},{19,... | collective-permute-start | bytes 3538952 | tf_op jit(solution)/shard_map/ppermute | solution.py:157
  14.4 50.4 %collective-permute-start.5 = (bf16[2,384,768]{2,1,0:T(8,128)(2,1)S(1)}, bf16[2,384,768]{2,1,0:T(8,128)(2,1)S(1)}, u32[]{:S(2)}, u32[]{:S(2)}) collective-permute-start(bf16[2,384,768]{2,1,0:T(8,128)(2,1)S(1)} %get-tuple-element.30), channel_id=1, source_target_pairs={{0,2},{3,1},{4,6},{7,5},{8,10},{11,9},{12,14},{15,13},{16,18},{19,... | collective-permute-start | bytes 3538952 | tf_op jit(solution)/shard_map/ppermute | solution.py:157
  40.7 27.6 %collective-permute-start.4 = (bf16[2,384,768]{2,1,0:T(8,128)(2,1)S(1)}, bf16[2,384,768]{2,1,0:T(8,128)(2,1)S(1)}, u32[]{:S(2)}, u32[]{:S(2)}) collective-permute-start(bf16[2,384,768]{2,1,0:T(8,128)(2,1)S(1)} %collective-permute-done.3), channel_id=1, source_target_pairs={{2,3},{1,0},{6,7},{5,4},{10,11},{9,8},{14,15},{13,12},{18,19},{17,... | collective-permute-start | bytes 3538952 | tf_op jit(solution)/shard_map/ppermute | solution.py:162
  64.8 28.8 %collective-permute-start.6 = (bf16[2,384,768]{2,1,0:T(8,128)(2,1)S(1)}, bf16[2,384,768]{2,1,0:T(8,128)(2,1)}, u32[]{:S(2)}, u32[]{:S(2)}) collective-permute-start(bf16[2,384,768]{2,1,0:T(8,128)(2,1)S(1)} %collective-permute-done.5), channel_id=1, source_target_pairs={{2,3},{1,0},{6,7},{5,4},{10,11},{9,8},{14,15},{13,12},{18,19},{17,... | collective-permute-start | bytes 3538952 | tf_op jit(solution)/shard_map/ppermute | solution.py:162
  96.7 1.3 copy-start.6
  96.7 1.3 copy-start.7
  115.2 102.2 %collective-permute-start = (bf16[4,384,768]{2,1,0:T(8,128)(2,1)S(1)}, bf16[4,384,768]{2,1,0:T(8,128)(2,1)}, u32[]{:S(2)}, u32[]{:S(2)}) collective-permute-start(bf16[4,384,768]{2,1,0:T(8,128)(2,1)S(1)} %first_section.6), channel_id=1, source_target_pairs={{0,1},{1,2},{2,3},{4,5},{5,6},{6,7},{8,9},{9,10},{10,11},{12,13},{... | collective-permute-start | bytes 7077896 | tf_op jit(solution)/shard_map/ppermute | solution.py:256
  124.0 93.4 %collective-permute-start.1 = (bf16[4,384,768]{2,1,0:T(8,128)(2,1)}, bf16[4,384,768]{2,1,0:T(8,128)(2,1)}, u32[]{:S(2)}, u32[]{:S(2)}) collective-permute-start(bf16[4,384,768]{2,1,0:T(8,128)(2,1)} %first_section.7), channel_id=1, source_target_pairs={{1,3},{2,0},{5,7},{6,4},{9,11},{10,8},{13,15},{14,12},{17,19},{18,... | collective-permute-start | bytes 7077896 | tf_op jit(solution)/shard_map/ppermute | solution.py:256
  125.3 7.1 %copy-start.11 = (s32[32,16]{0,1:T(8,128)S(1)}, s32[32,16]{0,1:T(8,128)}, u32[]{:S(2)}) copy-start(s32[32,16]{0,1:T(8,128)} %param.20) | copy-start | bytes 6148
  125.3 7.1 %copy-start.12 = (s32[32,16]{0,1:T(8,128)S(1)}, s32[32,16]{0,1:T(8,128)}, u32[]{:S(2)}) copy-start(s32[32,16]{0,1:T(8,128)} %param.19) | copy-start | bytes 6148
  130.1 101.4 %collective-permute-start.2 = (bf16[4,384,768]{2,1,0:T(8,128)(2,1)}, bf16[4,384,768]{2,1,0:T(8,128)(2,1)}, u32[]{:S(2)}, u32[]{:S(2)}) collective-permute-start(bf16[4,384,768]{2,1,0:T(8,128)(2,1)} %first_section.8), channel_id=1, source_target_pairs={{1,0},{2,1},{3,2},{5,4},{6,5},{7,6},{9,8},{10,9},{11,10},{13,12},{... | collective-permute-start | bytes 7077896 | tf_op jit(solution)/shard_map/ppermute | solution.py:256
  138.4 1.4 copy-start.2
  211.3 20.2 %copy-start.3 = (bf16[4,384,768]{2,1,0:T(8,128)(2,1)S(1)}, bf16[4,384,768]{2,1,0:T(8,128)(2,1)}, u32[]{:S(2)}) copy-start(bf16[4,384,768]{2,1,0:T(8,128)(2,1)} %copy-done.2) | copy-start | bytes 7077892
  216.0 1.4 copy-start.4
  247.5 15.1 %collective-permute-start.8 = (bf16[1,384,768]{2,1,0:T(8,128)(2,1)S(1)}, bf16[1,384,768]{2,1,0:T(8,128)(2,1)S(1)}, u32[]{:S(2)}, u32[]{:S(2)}) collective-permute-start(bf16[1,384,768]{2,1,0:T(8,128)(2,1)S(1)} %get-tuple-element.11), channel_id=1, source_target_pairs={{0,1},{3,2},{4,5},{7,6},{8,9},{11,10},{12,13},{15,14},{16,17},{19,... | collective-permute-start | bytes 1769480 | tf_op jit(solution)/shard_map/ppermute | solution.py:275
  248.8 26.4 %collective-permute-start.10 = (bf16[1,384,768]{2,1,0:T(8,128)(2,1)S(1)}, bf16[1,384,768]{2,1,0:T(8,128)(2,1)S(1)}, u32[]{:S(2)}, u32[]{:S(2)}) collective-permute-start(bf16[1,384,768]{2,1,0:T(8,128)(2,1)S(1)} %get-tuple-element.12), channel_id=1, source_target_pairs={{0,1},{3,2},{4,5},{7,6},{8,9},{11,10},{12,13},{15,14},{16,17},{19,... | collective-permute-start | bytes 1769480 | tf_op jit(solution)/shard_map/ppermute | solution.py:276
  250.2 33.6 %collective-permute-start.7 = (bf16[1,384,768]{2,1,0:T(8,128)(2,1)S(1)}, bf16[1,384,768]{2,1,0:T(8,128)(2,1)S(1)}, u32[]{:S(2)}, u32[]{:S(2)}) collective-permute-start(bf16[1,384,768]{2,1,0:T(8,128)(2,1)S(1)} %get-tuple-element.10), channel_id=1, source_target_pairs={{0,1},{1,0},{2,3},{3,2},{4,5},{5,4},{6,7},{7,6},{8,9},{9,8},{10,11... | collective-permute-start | bytes 1769480 | tf_op jit(solution)/shard_map/ppermute | solution.py:277
  262.7 21.1 %collective-permute-start.9 = (bf16[1,384,768]{2,1,0:T(8,128)(2,1)S(1)}, bf16[1,384,768]{2,1,0:T(8,128)(2,1)S(1)}, u32[]{:S(2)}, u32[]{:S(2)}) collective-permute-start(bf16[1,384,768]{2,1,0:T(8,128)(2,1)S(1)} %add_convert_fusion.1), channel_id=1, source_target_pairs={{1,3},{2,0},{5,7},{6,4},{9,11},{10,8},{13,15},{14,12},{17,19},{18,... | collective-permute-start | bytes 1769480 | tf_op jit(solution)/shard_map/ppermute | solution.py:280
  275.4 8.5 %collective-permute-start.11 = (bf16[1,384,768]{2,1,0:T(8,128)(2,1)S(1)}, bf16[1,384,768]{2,1,0:T(8,128)(2,1)S(1)}, u32[]{:S(2)}, u32[]{:S(2)}) collective-permute-start(bf16[1,384,768]{2,1,0:T(8,128)(2,1)S(1)} %add_convert_fusion), channel_id=1, source_target_pairs={{1,2},{2,1},{5,6},{6,5},{9,10},{10,9},{13,14},{14,13},{17,18},{18,... | collective-permute-start | bytes 1769480 | tf_op jit(solution)/shard_map/ppermute | solution.py:281
  283.8 1.3 copy-start.1
  (4 other events, 3.6 us)
Sparse Core Ops, SparseCore 0:
  9.2 101.4 all-gather.2
  112.6 98.7 all-gather.4

commit v5 on v4

--- a/solution.py
+++ b/solution.py
@@ -246,7 +246,7 @@
         )
 
     regions = [None] * (group_count + 1)
-    for turn in sorted(range(1, group_count), key=lambda j: -min(j, group_count - j)):
+    for turn in sorted(range(1, group_count), key=lambda j: min(j, group_count - j)):
         pairs = [
             (source, (source + turn) % group_count)
             for source in range(group_count)

time: 295 us -> 297 us (level)
  Pallas kernels: 40.3 us -> 32 us
  starting transfers between devices: 20.8 us -> 27.6 us
    pallas_call x1, Pallas kernels: 15.9 us -> 9.37 us  [second_sums(): pl.pallas_call(lambda *refs: second_kernel(len(regions), norm_factor, *re...]
    ppermute x1, starting transfers between devices: 1.33 us -> 7.82 us  [body(): end_came = lax.ppermute(sums[0], 'ops', inward)]
where the time goes in v5:
time: 297 us; the launch traced here: 293 us
  waiting for transfers between devices  206 us (69%)
  Pallas kernels  32 us (11%)
  starting transfers between devices  27.6 us (9%)
  between operations  13.8 us (5%)
  other arithmetic  7.22 us (2%)
  local copies, waits for them, and re-layouts  6.18 us (2%)
    all_gather x1, waiting for transfers between devices, body(): far_rows = lax.all_gather(far_nodes, 'tm', axis=0, tiled=True)  71.7 us
    ppermute x2, waiting for transfers between devices, body(): lax.ppermute(pieces[cut], 'ops', [(0, half), (group_count - 1, half - 1)])  47.8 us
    ppermute x2, waiting for transfers between devices, body(): chains[cut].append(lax.ppermute(chains[cut][-1], 'ops', onward))  27.4 us
    pallas_call x5, Pallas kernels, first_products(): pl.pallas_call(lambda *refs: first_kernel(norm_factor, *refs), grid_spec=...  22.6 us
    ppermute x3, waiting for transfers between devices, body(): regions[turn] = lax.ppermute(near_products(turn), 'ops', pairs)  15.9 us
    ppermute x1, waiting for transfers between devices, body(): end_came = lax.ppermute(sums[0], 'ops', inward)  12.3 us
    ppermute x1, waiting for transfers between devices, body(): inner_came = lax.ppermute(sums[1], 'ops', inward)  11.2 us
    all_gather x1, waiting for transfers between devices, body(): near_rows = lax.all_gather(node_blocks, 'tm', axis=0, tiled=True)  10.9 us
  transfers between devices with their start and end apart: 14, of which 10 were waited for; matrix products, arithmetic and copies ran while one was open for 3% of the time, Pallas kernels for 8%

profile of v5, /device:TPU:0, one launch (start us, length us, event | category | flops | bytes accessed | tf_op | source)
XLA Modules:
  0.0 293.0 jit_solution(1751516865089874313)
XLA Ops:
  8.4 6.0 %collective-permute-start.3 = (bf16[2,384,768]{2,1,0:T(8,128)(2,1)S(1)}, bf16[2,384,768]{2,1,0:T(8,128)(2,1)S(1)}, u32[]{:S(2)}, u32[]{:S(2)}) collective-permute-start(bf16[2,384,768]{2,1,0:T(8,128)(2,1)S(1)} %get-tuple-element.29), channel_id=1, source_target_pairs={{0,2},{3,1},{4,6},{7,5},{8,10},{11,9},{12,14},{15,13},{16,18},{19,... | collective-permute-start | bytes 3538952 | tf_op jit(solution)/shard_map/ppermute | solution.py:157
  14.4 1.4 collective-permute-start.5
  15.8 24.9 %collective-permute-done.3 = bf16[2,384,768]{2,1,0:T(8,128)(2,1)S(1)} collective-permute-done((bf16[2,384,768]{2,1,0:T(8,128)(2,1)S(1)}, bf16[2,384,768]{2,1,0:T(8,128)(2,1)S(1)}, u32[]{:S(2)}, u32[]{:S(2)}) %collective-permute-start.3) | collective-permute-done | bytes 1179680 | tf_op jit(solution)/shard_map/ppermute | solution.py:157
  42.0 22.8 %collective-permute-done.5 = bf16[2,384,768]{2,1,0:T(8,128)(2,1)S(1)} collective-permute-done((bf16[2,384,768]{2,1,0:T(8,128)(2,1)S(1)}, bf16[2,384,768]{2,1,0:T(8,128)(2,1)S(1)}, u32[]{:S(2)}, u32[]{:S(2)}) %collective-permute-start.5) | collective-permute-done | bytes 1179680 | tf_op jit(solution)/shard_map/ppermute | solution.py:157
  66.1 2.1 collective-permute-done.4
  68.4 25.3 %collective-permute-done.6 = bf16[2,384,768]{2,1,0:T(8,128)(2,1)} collective-permute-done((bf16[2,384,768]{2,1,0:T(8,128)(2,1)S(1)}, bf16[2,384,768]{2,1,0:T(8,128)(2,1)}, u32[]{:S(2)}, u32[]{:S(2)}) %collective-permute-start.6) | collective-permute-done | bytes 1179680 | tf_op jit(solution)/shard_map/ppermute | solution.py:162
  93.6 1.4 broadcast_select_fusion
  95.1 1.6 pad_maximum_fusion
  99.8 10.9 %all-gather.3.cloned.1.call-done.refs_3_.refs_4_ = bf16[32,384,768]{2,1,0:T(8,128)(2,1)} async-done(((bf16[4,384,768]{2,1,0:T(8,128)(2,1)}), bf16[32,384,768]{2,1,0:T(8,128)(2,1)}) %all-gather.3.cloned.1.call-update) | async-done | bytes 18874384 | tf_op jit(solution)/shard_map/all_gather | solution.py:152
  110.7 5.4 %first_section.6 = bf16[4,384,768]{2,1,0:T(8,128)(2,1)S(1)} custom-call(s32[4]{0:T(128)S(1)} %get-tuple-element.43.refs_0_, s32[4]{0:T(128)S(1)} %get-tuple-element.39.refs_1_, s32[4]{0:T(128)S(1)} %get-tuple-element.35.refs_2_, bf16[32,384,768]{2,1,0:T(8,128)(2,1)} %all-gather.3.cloned.1.call-done.refs_3_.refs_4_, ...), custom_call_target="tpu_custom_call" | custom-call | flops 1811939328 | bytes 7077888 | tf_op jit(solution)/shard_map/first_section/pallas_call | solution.py:66
  116.1 3.8 %collective-permute-start = (bf16[4,384,768]{2,1,0:T(8,128)(2,1)S(1)}, bf16[4,384,768]{2,1,0:T(8,128)(2,1)}, u32[]{:S(2)}, u32[]{:S(2)}) collective-permute-start(bf16[4,384,768]{2,1,0:T(8,128)(2,1)S(1)} %first_section.6), channel_id=1, source_target_pairs={{0,1},{1,2},{2,3},{4,5},{5,6},{6,7},{8,9},{9,10},{10,11},{12,13},{... | collective-permute-start | bytes 7077896 | tf_op jit(solution)/shard_map/ppermute | solution.py:256
  120.0 4.9 %first_section.7 = bf16[4,384,768]{2,1,0:T(8,128)(2,1)} custom-call(s32[4]{0:T(128)S(1)} %get-tuple-element.42.refs_0_, s32[4]{0:T(128)S(1)} %get-tuple-element.38.refs_1_, s32[4]{0:T(128)S(1)} %get-tuple-element.34.refs_2_, bf16[32,384,768]{2,1,0:T(8,128)(2,1)} %all-gather.3.cloned.1.call-done.refs_3_.refs_4_, ...), custom_call_target="tpu_custom_call" | custom-call | flops 1811939328 | bytes 7077888 | tf_op jit(solution)/shard_map/first_section/pallas_call | solution.py:66
  126.2 4.8 %first_section.8 = bf16[4,384,768]{2,1,0:T(8,128)(2,1)} custom-call(s32[4]{0:T(128)S(1)} %get-tuple-element.41.refs_0_, s32[4]{0:T(128)S(1)} %get-tuple-element.37.refs_1_, s32[4]{0:T(128)S(1)} %get-tuple-element.33.refs_2_, bf16[32,384,768]{2,1,0:T(8,128)(2,1)} %all-gather.3.cloned.1.call-done.refs_3_.refs_4_, ...), custom_call_target="tpu_custom_call" | custom-call | flops 1811939328 | bytes 7077888 | tf_op jit(solution)/shard_map/first_section/pallas_call | solution.py:66
  134.2 4.1 %first_section.5.refs_5_ = bf16[4,384,768]{2,1,0:T(8,128)(2,1)S(1)} custom-call(s32[4]{0:T(128)S(1)} %get-tuple-element.44.refs_0_, s32[4]{0:T(128)S(1)} %get-tuple-element.40.refs_1_, s32[4]{0:T(128)S(1)} %get-tuple-element.36.refs_2_, bf16[32,384,768]{2,1,0:T(8,128)(2,1)} %all-gather.3.cloned.1.call-done.refs_3_.refs_4_, ...), custom_call_target="tpu_custom_call" | custom-call | flops 1811939328 | bytes 7077888 | tf_op jit(solution)/shard_map/first_section/pallas_call | solution.py:66
  138.3 1.4 copy-done.2
  139.7 71.7 %all-gather.5.cloned.1.call-done.refs_3_.refs_4_ = bf16[32,384,768]{2,1,0:T(8,128)(2,1)} async-done(((bf16[4,384,768]{2,1,0:T(8,128)(2,1)}), bf16[32,384,768]{2,1,0:T(8,128)(2,1)}) %all-gather.5.cloned.1.call-update) | async-done | bytes 18874384 | tf_op jit(solution)/shard_map/all_gather | solution.py:172
  211.3 3.4 %first_section.9.refs_9_ = bf16[4,384,768]{2,1,0:T(8,128)(2,1)S(1)} custom-call(s32[4]{0:T(128)S(1)} %get-tuple-element.22.refs_0_, s32[4]{0:T(128)S(1)} %get-tuple-element.21.refs_1_, s32[4]{0:T(128)S(1)} %convert_element_type.41.refs_2_, bf16[32,384,768]{2,1,0:T(8,128)(2,1)} %all-gather.5.cloned.1.call-done.refs_3_.refs_4_, ...), custom_call_target="tpu_custom_call" | custom-call | flops 1811939328 | bytes 7077888 | tf_op jit(solution)/shard_map/first_section/pallas_call | solution.py:66
  214.7 1.4 copy-done.4
  216.1 15.9 %collective-permute-done.2.refs_8_ = bf16[4,384,768]{2,1,0:T(8,128)(2,1)} collective-permute-done((bf16[4,384,768]{2,1,0:T(8,128)(2,1)}, bf16[4,384,768]{2,1,0:T(8,128)(2,1)}, u32[]{:S(2)}, u32[]{:S(2)}) %collective-permute-start.2) | collective-permute-done | bytes 2359328 | tf_op jit(solution)/shard_map/ppermute | solution.py:256
  232.0 9.4 %second_section.1 = (bf16[1,384,768]{2,1,0:T(8,128)(2,1)S(1)}, bf16[1,384,768]{2,1,0:T(8,128)(2,1)S(1)}, bf16[1,384,768]{2,1,0:T(8,128)(2,1)S(1)}, f32[1,384,768]{2,1,0:T(8,128)S(1)}) custom-call(s32[16]{0:T(128)S(1)} %get-tuple-element.28.refs_0_, s32[16]{0:T(128)S(1)} %get-tuple-element.27.refs_1_, s32[16]{0:T(128)S(1)} %compare_select_fusion.6.refs_2_, ...), custom_call_target="tpu_custom_call" | custom-call | flops 7247757312 | bytes 28311552 | tf_op jit(solution)/shard_map/second_section/pallas_call | solution.py:91
  241.3 7.8 %collective-permute-start.8 = (bf16[1,384,768]{2,1,0:T(8,128)(2,1)S(1)}, bf16[1,384,768]{2,1,0:T(8,128)(2,1)S(1)}, u32[]{:S(2)}, u32[]{:S(2)}) collective-permute-start(bf16[1,384,768]{2,1,0:T(8,128)(2,1)S(1)} %get-tuple-element.11), channel_id=1, source_target_pairs={{0,1},{3,2},{4,5},{7,6},{8,9},{11,10},{12,13},{15,14},{16,17},{19,... | collective-permute-start | bytes 1769480 | tf_op jit(solution)/shard_map/ppermute | solution.py:275
  250.6 12.3 %collective-permute-done.8 = bf16[1,384,768]{2,1,0:T(8,128)(2,1)S(1)} collective-permute-done((bf16[1,384,768]{2,1,0:T(8,128)(2,1)S(1)}, bf16[1,384,768]{2,1,0:T(8,128)(2,1)S(1)}, u32[]{:S(2)}, u32[]{:S(2)}) %collective-permute-start.8) | collective-permute-done | bytes 589856 | tf_op jit(solution)/shard_map/ppermute | solution.py:275
  264.4 11.2 %collective-permute-done.10 = bf16[1,384,768]{2,1,0:T(8,128)(2,1)S(1)} collective-permute-done((bf16[1,384,768]{2,1,0:T(8,128)(2,1)S(1)}, bf16[1,384,768]{2,1,0:T(8,128)(2,1)S(1)}, u32[]{:S(2)}, u32[]{:S(2)}) %collective-permute-start.10) | collective-permute-done | bytes 589856 | tf_op jit(solution)/shard_map/ppermute | solution.py:276
  276.4 8.5 %collective-permute-done.7 = bf16[1,384,768]{2,1,0:T(8,128)(2,1)S(1)} collective-permute-done((bf16[1,384,768]{2,1,0:T(8,128)(2,1)S(1)}, bf16[1,384,768]{2,1,0:T(8,128)(2,1)S(1)}, u32[]{:S(2)}, u32[]{:S(2)}) %collective-permute-start.7) | collective-permute-done | bytes 589856 | tf_op jit(solution)/shard_map/ppermute | solution.py:277
  (90 shorter events, 16.9 us)
Async XLA Ops:
  6.5 90.9 %copy-start = (s32[32,16]{0,1:T(8,128)S(1)}, s32[32,16]{0,1:T(8,128)}, u32[]{:S(2)}) copy-start(s32[32,16]{0,1:T(8,128)} %param.15) | copy-start | bytes 6148
  6.5 1.7 copy-start.5
  6.5 104.2 %all-gather.3.cloned.1.call-start = ((), (), s32[]{:S(2)}) async-start(), calls=%async_computation | async-start | bytes 21233664 | tf_op jit(solution)/shard_map/all_gather | solution.py:152
  7.3 204.1 %all-gather.5.cloned.1.call-start = ((), (), s32[]{:S(2)}) async-start(), calls=%async_computation.1 | async-start | bytes 21233664 | tf_op jit(solution)/shard_map/all_gather | solution.py:172
  8.4 32.3 %collective-permute-start.3 = (bf16[2,384,768]{2,1,0:T(8,128)(2,1)S(1)}, bf16[2,384,768]{2,1,0:T(8,128)(2,1)S(1)}, u32[]{:S(2)}, u32[]{:S(2)}) collective-permute-start(bf16[2,384,768]{2,1,0:T(8,128)(2,1)S(1)} %get-tuple-element.29), channel_id=1, source_target_pairs={{0,2},{3,1},{4,6},{7,5},{8,10},{11,9},{12,14},{15,13},{16,18},{19,... | collective-permute-start | bytes 3538952 | tf_op jit(solution)/shard_map/ppermute | solution.py:157
  14.4 50.4 %collective-permute-start.5 = (bf16[2,384,768]{2,1,0:T(8,128)(2,1)S(1)}, bf16[2,384,768]{2,1,0:T(8,128)(2,1)S(1)}, u32[]{:S(2)}, u32[]{:S(2)}) collective-permute-start(bf16[2,384,768]{2,1,0:T(8,128)(2,1)S(1)} %get-tuple-element.30), channel_id=1, source_target_pairs={{0,2},{3,1},{4,6},{7,5},{8,10},{11,9},{12,14},{15,13},{16,18},{19,... | collective-permute-start | bytes 3538952 | tf_op jit(solution)/shard_map/ppermute | solution.py:157
  40.7 27.6 %collective-permute-start.4 = (bf16[2,384,768]{2,1,0:T(8,128)(2,1)S(1)}, bf16[2,384,768]{2,1,0:T(8,128)(2,1)S(1)}, u32[]{:S(2)}, u32[]{:S(2)}) collective-permute-start(bf16[2,384,768]{2,1,0:T(8,128)(2,1)S(1)} %collective-permute-done.3), channel_id=1, source_target_pairs={{2,3},{1,0},{6,7},{5,4},{10,11},{9,8},{14,15},{13,12},{18,19},{17,... | collective-permute-start | bytes 3538952 | tf_op jit(solution)/shard_map/ppermute | solution.py:162
  64.8 28.8 %collective-permute-start.6 = (bf16[2,384,768]{2,1,0:T(8,128)(2,1)S(1)}, bf16[2,384,768]{2,1,0:T(8,128)(2,1)}, u32[]{:S(2)}, u32[]{:S(2)}) collective-permute-start(bf16[2,384,768]{2,1,0:T(8,128)(2,1)S(1)} %collective-permute-done.5), channel_id=1, source_target_pairs={{2,3},{1,0},{6,7},{5,4},{10,11},{9,8},{14,15},{13,12},{18,19},{17,... | collective-permute-start | bytes 3538952 | tf_op jit(solution)/shard_map/ppermute | solution.py:162
  96.7 1.3 copy-start.6
  96.7 1.3 copy-start.7
  116.1 100.0 %collective-permute-start = (bf16[4,384,768]{2,1,0:T(8,128)(2,1)S(1)}, bf16[4,384,768]{2,1,0:T(8,128)(2,1)}, u32[]{:S(2)}, u32[]{:S(2)}) collective-permute-start(bf16[4,384,768]{2,1,0:T(8,128)(2,1)S(1)} %first_section.6), channel_id=1, source_target_pairs={{0,1},{1,2},{2,3},{4,5},{5,6},{6,7},{8,9},{9,10},{10,11},{12,13},{... | collective-permute-start | bytes 7077896 | tf_op jit(solution)/shard_map/ppermute | solution.py:256
  124.9 91.2 %collective-permute-start.1 = (bf16[4,384,768]{2,1,0:T(8,128)(2,1)}, bf16[4,384,768]{2,1,0:T(8,128)(2,1)}, u32[]{:S(2)}, u32[]{:S(2)}) collective-permute-start(bf16[4,384,768]{2,1,0:T(8,128)(2,1)} %first_section.7), channel_id=1, source_target_pairs={{1,3},{2,0},{5,7},{6,4},{9,11},{10,8},{13,15},{14,12},{17,19},{18,... | collective-permute-start | bytes 7077896 | tf_op jit(solution)/shard_map/ppermute | solution.py:256
  126.1 7.1 %copy-start.11 = (s32[32,16]{0,1:T(8,128)S(1)}, s32[32,16]{0,1:T(8,128)}, u32[]{:S(2)}) copy-start(s32[32,16]{0,1:T(8,128)} %param.20) | copy-start | bytes 6148
  126.2 7.1 %copy-start.12 = (s32[32,16]{0,1:T(8,128)S(1)}, s32[32,16]{0,1:T(8,128)}, u32[]{:S(2)}) copy-start(s32[32,16]{0,1:T(8,128)} %param.19) | copy-start | bytes 6148
  131.0 100.9 %collective-permute-start.2 = (bf16[4,384,768]{2,1,0:T(8,128)(2,1)}, bf16[4,384,768]{2,1,0:T(8,128)(2,1)}, u32[]{:S(2)}, u32[]{:S(2)}) collective-permute-start(bf16[4,384,768]{2,1,0:T(8,128)(2,1)} %first_section.8), channel_id=1, source_target_pairs={{1,0},{2,1},{3,2},{5,4},{6,5},{7,6},{9,8},{10,9},{11,10},{13,12},{... | collective-permute-start | bytes 7077896 | tf_op jit(solution)/shard_map/ppermute | solution.py:256
  138.3 1.4 copy-start.2
  211.3 20.6 %copy-start.3 = (bf16[4,384,768]{2,1,0:T(8,128)(2,1)S(1)}, bf16[4,384,768]{2,1,0:T(8,128)(2,1)}, u32[]{:S(2)}) copy-start(bf16[4,384,768]{2,1,0:T(8,128)(2,1)} %copy-done.2) | copy-start | bytes 7077892
  214.7 1.4 copy-start.4
  241.3 21.6 %collective-permute-start.8 = (bf16[1,384,768]{2,1,0:T(8,128)(2,1)S(1)}, bf16[1,384,768]{2,1,0:T(8,128)(2,1)S(1)}, u32[]{:S(2)}, u32[]{:S(2)}) collective-permute-start(bf16[1,384,768]{2,1,0:T(8,128)(2,1)S(1)} %get-tuple-element.11), channel_id=1, source_target_pairs={{0,1},{3,2},{4,5},{7,6},{8,9},{11,10},{12,13},{15,14},{16,17},{19,... | collective-permute-start | bytes 1769480 | tf_op jit(solution)/shard_map/ppermute | solution.py:275
  249.2 26.4 %collective-permute-start.10 = (bf16[1,384,768]{2,1,0:T(8,128)(2,1)S(1)}, bf16[1,384,768]{2,1,0:T(8,128)(2,1)S(1)}, u32[]{:S(2)}, u32[]{:S(2)}) collective-permute-start(bf16[1,384,768]{2,1,0:T(8,128)(2,1)S(1)} %get-tuple-element.12), channel_id=1, source_target_pairs={{0,1},{3,2},{4,5},{7,6},{8,9},{11,10},{12,13},{15,14},{16,17},{19,... | collective-permute-start | bytes 1769480 | tf_op jit(solution)/shard_map/ppermute | solution.py:276
  250.5 34.4 %collective-permute-start.7 = (bf16[1,384,768]{2,1,0:T(8,128)(2,1)S(1)}, bf16[1,384,768]{2,1,0:T(8,128)(2,1)S(1)}, u32[]{:S(2)}, u32[]{:S(2)}) collective-permute-start(bf16[1,384,768]{2,1,0:T(8,128)(2,1)S(1)} %get-tuple-element.10), channel_id=1, source_target_pairs={{0,1},{1,0},{2,3},{3,2},{4,5},{5,4},{6,7},{7,6},{8,9},{9,8},{10,11... | collective-permute-start | bytes 1769480 | tf_op jit(solution)/shard_map/ppermute | solution.py:277
  263.1 21.8 %collective-permute-start.9 = (bf16[1,384,768]{2,1,0:T(8,128)(2,1)S(1)}, bf16[1,384,768]{2,1,0:T(8,128)(2,1)S(1)}, u32[]{:S(2)}, u32[]{:S(2)}) collective-permute-start(bf16[1,384,768]{2,1,0:T(8,128)(2,1)S(1)} %add_convert_fusion.1), channel_id=1, source_target_pairs={{1,3},{2,0},{5,7},{6,4},{9,11},{10,8},{13,15},{14,12},{17,19},{18,... | collective-permute-start | bytes 1769480 | tf_op jit(solution)/shard_map/ppermute | solution.py:280
  275.7 9.2 %collective-permute-start.11 = (bf16[1,384,768]{2,1,0:T(8,128)(2,1)S(1)}, bf16[1,384,768]{2,1,0:T(8,128)(2,1)S(1)}, u32[]{:S(2)}, u32[]{:S(2)}) collective-permute-start(bf16[1,384,768]{2,1,0:T(8,128)(2,1)S(1)} %add_convert_fusion), channel_id=1, source_target_pairs={{1,2},{2,1},{5,6},{6,5},{9,10},{10,9},{13,14},{14,13},{17,18},{18,... | collective-permute-start | bytes 1769480 | tf_op jit(solution)/shard_map/ppermute | solution.py:281
  284.9 1.3 copy-start.1
  (4 other events, 3.6 us)
Sparse Core Ops, SparseCore 0:
  9.2 101.4 all-gather.2
  112.6 98.7 all-gather.4
